TPU v7x, 32 devices: a whole 2x2x4 slice. The times are simulated.
32 devices in a mesh: groups: 2 (over x), tm: 16 (over z, y, core).
Axes of the slice: x: 2, y: 2, z: 4, core: 2. Of those that a mesh axis runs over, the one named last changes fastest.
Arguments:
- observations: float32 [32, 8192], P(('groups', 'tm')), parts along dimension 0, may hold values from -6 to 6
- block_mask: int32 [32, 64], P(('groups', 'tm')), parts along dimension 0, may hold values 0 or 1
- block_of_sensor: int32 [8192], replicated, may hold values from 0 to 63
- sensor_basis: float32 [8192, 128], replicated, may hold values from -0.0625 to 0.0625
- noise_var: float32 [8192], replicated, may hold values from 0.25 to 1
- mode_rate: float32 [128], replicated, may hold values from 0.015 to 1
- mode_var: float32 [128], replicated, may hold values from 0.5 to 2
Outputs:
- field: float32 [32, 8192], P(('groups', 'tm')), parts along dimension 0
- variances: float32 [32, 256], P(('groups', 'tm')), parts along dimension 0
- misfit: float32 [2], P('groups'), parts along dimension 0
There are 2 independent parts, one for each index of `groups`. A program takes and returns all parts, laid end to end along the dimension named above; an argument that names none is the same for every part. Nothing has to cross between parts.
All inputs are finite; a program needn't handle non-finite values. No bound on the sum of `block_mask` on one device may be relied on, other than what follows from the above.
Results may differ from a plain program's by a relative error of at most 0.0003.
Values sent between devices are 32-bit elements; how exact they have to be, the bound alone decides.
No kernel may reach another device: no remote copies, remote signals or barrier semaphores. Data moves between devices by JAX's collectives and lax.ppermute only.
A program may use at most 128 MiB of HBM per device.

v0:
```python
import jax
import jax.numpy as jnp
from jax import lax
from jax.sharding import PartitionSpec as P


def entering(array, axis, combine, identity):
    count, index = (lax.axis_size(axis), lax.axis_index(axis))
    everything = jax.tree.map(lambda part: lax.all_gather(part, axis), array)
    start = jax.tree.map(
        lambda part, zero: jnp.broadcast_to(jnp.asarray(zero, part.dtype), part.shape),
        array,
        identity,
    )

    def lap(k, before):
        reached = k < index
        new = combine(before, jax.tree.map(lambda part: part[k], everything))
        return jax.tree.map(lambda a, b: jnp.where(reached, a, b), new, before)

    return lax.fori_loop(0, count, lap, start)


def matmul(left, right):
    return jnp.dot(left, right, precision=lax.Precision.HIGHEST, preferred_element_type=jnp.float32)


def transition(mode_rate, mode_var):
    doubled = 2.0 * mode_rate
    damping = jnp.exp(-doubled)
    term_now = doubled * doubled * doubled / 6.0
    series = term_now
    for order in range(4, 15):
        term_now = term_now * doubled / order
        series = series + term_now
    q_value = mode_var * damping * series
    q_rate = mode_var * damping * (2.0 * doubled + series)
    q_cross = mode_var * damping * 2.0 * mode_rate * mode_rate
    root_value = jnp.sqrt(q_value)
    root_cross = q_cross / root_value
    root_rate = jnp.sqrt(q_value * q_rate - q_cross * q_cross) / root_value
    decay = jnp.exp(-mode_rate)
    return (
        decay * (1.0 + mode_rate),
        decay * mode_rate,
        -decay * mode_rate,
        decay * (1.0 - mode_rate),
        root_value,
        root_cross,
        root_rate,
        jnp.sqrt(mode_var),
    )


def build_element(info_mat, grad_vec, is_first, coefficients):
    f_vv, f_vr, f_rv, f_rr, root_value, root_cross, root_rate, sigma_vec = coefficients
    f_vv = jnp.where(is_first, 0.0, f_vv)
    f_vr = jnp.where(is_first, 0.0, f_vr)
    f_rv = jnp.where(is_first, 0.0, f_rv)
    f_rr = jnp.where(is_first, 0.0, f_rr)
    root_value = jnp.where(is_first, sigma_vec, root_value)
    root_cross = jnp.where(is_first, 0.0, root_cross)
    root_rate = jnp.where(is_first, sigma_vec, root_rate)
    modes = info_mat.shape[0]
    ident_modes = jnp.eye(modes, dtype=jnp.float32)
    inner = ident_modes + root_value[:, None] * info_mat * root_value[None, :]
    factor_m = jnp.linalg.cholesky(inner)
    solved = jax.scipy.linalg.solve_triangular(factor_m, ident_modes, lower=True)
    inverse = matmul(solved.T, solved)
    cov_vv = root_value[:, None] * inverse * root_value[None, :]
    cov_vr = root_value[:, None] * inverse * root_cross[None, :]
    cov_rr = root_cross[:, None] * inverse * root_cross[None, :] + jnp.diag(root_rate * root_rate)
    covar = jnp.block([[cov_vv, cov_vr], [cov_vr.T, cov_rr]])
    left_cols = covar[:, :modes]
    mean_vec = matmul(left_cols, grad_vec)
    kalman = matmul(left_cols, info_mat)
    ident_state = jnp.eye(2 * modes, dtype=jnp.float32)
    remain = ident_state - jnp.concatenate(
        [kalman, jnp.zeros((2 * modes, modes), jnp.float32)], axis=1
    )
    trans_mat = jnp.concatenate(
        [
            remain[:, :modes] * f_vv[None, :] + remain[:, modes:] * f_rv[None, :],
            remain[:, :modes] * f_vr[None, :] + remain[:, modes:] * f_rr[None, :],
        ],
        axis=1,
    )
    info_left = info_mat - matmul(info_mat, kalman[:modes])
    scale_vec = jnp.concatenate([f_vv, f_vr])
    precis = scale_vec[:, None] * jnp.tile(info_left, (2, 2)) * scale_vec[None, :]
    grad_left = grad_vec - matmul(info_mat, mean_vec[:modes])
    eta_vec = jnp.concatenate([f_vv * grad_left, f_vr * grad_left])
    return (trans_mat, mean_vec, covar, eta_vec, precis, jnp.ones((), jnp.float32))


def make_identity(state):
    return (
        jnp.eye(state, dtype=jnp.float32),
        jnp.zeros((state,), jnp.float32),
        jnp.zeros((state, state), jnp.float32),
        jnp.zeros((state,), jnp.float32),
        jnp.zeros((state, state), jnp.float32),
        jnp.zeros((), jnp.float32),
    )


def solve_parts(covar_a, live_a, precis_b):
    state = covar_a.shape[0]
    ident_state = jnp.eye(state, dtype=jnp.float32)
    factor_c = jnp.linalg.cholesky(covar_a + (1.0 - live_a) * ident_state)
    left_prod = matmul(factor_c.T, precis_b)
    middle = ident_state + matmul(left_prod, factor_c)
    factor_m = jnp.linalg.cholesky(middle)
    whitened = jax.scipy.linalg.solve_triangular(factor_m, factor_c.T, lower=True)
    return ident_state - matmul(matmul(whitened.T, whitened), precis_b)


def combine(earlier, later):
    trans_a, mean_a, covar_a, eta_a, precis_a, live_a = earlier
    trans_b, mean_b, covar_b, eta_b, precis_b, live_b = later
    inverse_x = solve_parts(covar_a, live_a, precis_b)
    forward = matmul(trans_b, inverse_x)
    new_trans = matmul(forward, trans_a)
    new_mean = matmul(forward, mean_a + matmul(covar_a, eta_b)) + mean_b
    new_covar = matmul(matmul(forward, covar_a), trans_b.T) + covar_b
    backward = matmul(inverse_x, trans_a).T
    new_eta = matmul(backward, eta_b - matmul(precis_b, mean_a)) + eta_a
    new_precis = matmul(matmul(backward, precis_b), trans_a) + precis_a
    keep = live_a > 0.5
    merged = (new_trans, new_mean, new_covar, new_eta, new_precis, jnp.maximum(live_a, live_b))
    return tuple((jnp.where(keep, new_part, old_part) for new_part, old_part in zip(merged, later)))


def apply_prefix(prefix, local_part):
    trans_a, mean_a, covar_a, eta_a, precis_a, live_a = prefix
    trans_b, mean_b, covar_b, eta_b, precis_b, live_b = local_part
    inverse_x = solve_parts(covar_a, live_a, precis_b)
    forward = matmul(trans_b, inverse_x)
    new_mean = matmul(forward, mean_a + matmul(covar_a, eta_b)) + mean_b
    new_covar = matmul(matmul(forward, covar_a), trans_b.T) + covar_b
    keep = live_a > 0.5
    return (jnp.where(keep, new_mean, mean_b), jnp.where(keep, new_covar, covar_b))


def on_device(
    observations, block_mask, block_of_sensor, sensor_basis, noise_var, mode_rate, mode_var
):
    steps_local, sensors = observations.shape
    modes = sensor_basis.shape[1]
    blocks = block_mask.shape[1]
    coefficients = transition(mode_rate, mode_var)
    onehot = (block_of_sensor[:, None] == jnp.arange(blocks, dtype=jnp.int32)[None, :]).astype(
        jnp.float32
    )
    observed = matmul(block_mask.astype(jnp.float32), onehot.T)
    weights = observed / noise_var[None, :]
    info_all = jnp.einsum(
        "sm,ks,sn->kmn",
        sensor_basis,
        weights,
        sensor_basis,
        precision=lax.Precision.HIGHEST,
        preferred_element_type=jnp.float32,
    )
    grad_all = matmul(weights * observations, sensor_basis)
    step_ids = lax.axis_index("tm") * steps_local + jnp.arange(steps_local, dtype=jnp.int32)
    firsts = step_ids == 0
    elements = jax.vmap(build_element, in_axes=(0, 0, 0, None))(
        info_all, grad_all, firsts, coefficients
    )
    identity = make_identity(2 * modes)

    def fold_step(carry, element):
        joined = combine(carry, element)
        return (joined, joined)

    first_element = tuple((part[0] for part in elements))
    rest_elements = tuple((part[1:] for part in elements))
    aggregate, rest_inclusive = lax.scan(fold_step, first_element, rest_elements)
    inclusive = tuple(
        (
            jnp.concatenate([head[None], tail], axis=0)
            for head, tail in zip(first_element, rest_inclusive)
        )
    )
    agg_trans, agg_mean, agg_covar, agg_eta, agg_precis, agg_live = aggregate
    prefix = entering(
        (agg_trans, agg_mean, agg_covar, agg_eta, agg_precis, agg_live), "tm", combine, identity
    )
    means, covars = jax.vmap(apply_prefix, in_axes=(None, 0))(prefix, inclusive)
    variances = jnp.diagonal(covars, axis1=1, axis2=2)
    field = matmul(means[:, :modes], sensor_basis.T)
    local_misfit = jnp.sum(weights * (observations - field) ** 2)
    total_misfit = lax.psum(local_misfit, "tm")
    misfit = (total_misfit / (steps_local * lax.axis_size("tm") * sensors)).reshape(1)
    return (field, variances, misfit)


def solution(mesh):
    in_specs = (P(("groups", "tm"), None), P(("groups", "tm"), None), P(), P(), P(), P(), P())
    out_specs = (P(("groups", "tm"), None), P(("groups", "tm"), None), P("groups"))
    return jax.shard_map(
        on_device, mesh=mesh, in_specs=in_specs, out_specs=out_specs, check_vma=False
    )
```

profile of v0, /device:TPU:1, one launch (start us, length us, event | category | flops | bytes accessed | tf_op | source)
XLA Modules:
  0.0 2138.2 jit_solution(16427149030474314338)
XLA Ops:
  10.9 11.8 fusion.63
  23.1 11.9 custom-call.43
  56.3 31.0 %all-reduce.3 = f32[16]{0:T(128)S(1)} all-reduce(f32[16]{0:T(128)S(1)} %dynamic-update-slice.27), channel_id=1, replica_groups=mesh['groups'=2,'tm'=16] {'tm'}, use_global_device_ids=true, to_apply=%add.3 | all-reduce | flops 16 | bytes 128
  87.3 21.5 %all-gather.1 = f32[16,1,256]{2,1,0:T(1,128)S(1)} all-gather(f32[1,1,256]{2,1,0:T(1,128)S(1)} %fusion.122), channel_id=1, replica_groups=mesh['groups'=2,'tm'=16] {'tm'}, dimensions={0}, use_global_device_ids=true | all-gather | bytes 17408 | tf_op jit(solution)/shard_map/all_gather | solution.py:9
  108.8 19.0 all-gather.2
  127.9 29.8 %all-gather.7.cloned.1.call-done = f32[16,256,256]{2,1,0:T(8,128)} async-done(((f32[1,256,256]{2,1,0:T(8,128)}), f32[16,256,256]{2,1,0:T(8,128)}) %all-gather.7.cloned.1.call-update) | async-done | bytes 4194320 | tf_op jit(solution)/shard_map/all_gather | solution.py:9
  157.7 51.3 %all-gather.11.cloned.1.call-done = f32[16,256,256]{2,1,0:T(8,128)} async-done(((f32[1,256,256]{2,1,0:T(8,128)}), f32[16,256,256]{2,1,0:T(8,128)}) %all-gather.11.cloned.1.call-update) | async-done | bytes 4194320 | tf_op jit(solution)/shard_map/all_gather | solution.py:9
  208.9 1780.5 %while.24 = (s32[]{:T(128)}, f32[256]{0:T(256)S(1)}, f32[256,256]{0,1:T(8,128)S(1)}, f32[]{:T(128)}, s32[]{:T(128)}, /*index=5*/f32[16,256,256]{2,1,0:T(8,128)},...) while((s32[]{:T(128)}, f32[256]{0:T(256)S(1)}, ...), condition=%wide.region_7.9_spmd.clone, body=%wide.region_2.8_spmd.clone.sunk | while | flops 1665533952 | bytes 17255904 | solution.py:21
  227.7 11.7 custom-call.79
  250.0 11.7 custom-call.81
  266.0 11.7 custom-call.82
  288.2 11.7 custom-call.84
  307.3 19.7 custom-call.86
  337.3 11.7 custom-call.79
  359.5 11.7 custom-call.81
  375.5 11.7 custom-call.82
  397.8 11.7 custom-call.84
  416.9 19.7 custom-call.86
  446.8 11.7 custom-call.79
  469.1 11.7 custom-call.81
  485.1 11.7 custom-call.82
  507.4 11.7 custom-call.84
  526.5 19.7 custom-call.86
  556.4 11.7 custom-call.79
  578.7 11.7 custom-call.81
  594.7 11.7 custom-call.82
  617.0 11.7 custom-call.84
  636.0 19.7 custom-call.86
  666.0 11.7 custom-call.79
  688.3 11.7 custom-call.81
  704.3 11.7 custom-call.82
  726.6 11.7 custom-call.84
  745.6 19.7 custom-call.86
  775.6 11.7 custom-call.79
  797.9 11.7 custom-call.81
  813.9 11.7 custom-call.82
  836.1 11.7 custom-call.84
  855.2 19.7 custom-call.86
  885.2 11.7 custom-call.79
  907.4 11.7 custom-call.81
  923.5 11.7 custom-call.82
  945.7 11.7 custom-call.84
  964.8 19.7 custom-call.86
  994.7 11.7 custom-call.79
  1017.0 11.7 custom-call.81
  1033.0 11.7 custom-call.82
  1055.3 11.7 custom-call.84
  1074.4 19.7 custom-call.86
  1104.3 11.7 custom-call.79
  1126.6 11.7 custom-call.81
  1183.9 19.7 custom-call.86
  1293.5 19.7 custom-call.86
  1403.1 19.7 custom-call.86
  1512.7 19.7 custom-call.86
  1622.3 19.7 custom-call.86
  1731.8 19.7 custom-call.86
  1841.4 19.7 custom-call.86
  1951.0 19.7 custom-call.86
  1989.7 11.7 custom-call.66
  2012.1 11.7 custom-call.68
  2027.0 11.9 custom-call.45
  2049.6 11.7 custom-call.47
  2068.0 19.9 custom-call.48
  2096.2 29.7 %psum.7 = f32[]{:T(128)} all-reduce(f32[]{:T(128)} %get-tuple-element.386), channel_id=1, replica_groups=mesh['groups'=2,'tm'=16] {'tm'}, use_global_device_ids=true, to_apply=%region_13.15 | all-reduce | flops 1 | bytes 8 | tf_op jit(solution)/shard_map/psum | solution.py:194
  (1164 shorter events, 1111.6 us)
Async XLA Ops:
  7.2 120.7 %all-gather.9.cloned.1.call-start = ((), (), s32[]{:S(2)}) async-start(), calls=%async_computation.1 | async-start | bytes 4456448 | tf_op jit(solution)/shard_map/all_gather | solution.py:9
  10.9 36.3 %copy-start.1 = (f32[1,8192]{1,0:T(1,128)S(1)}, f32[1,8192]{1,0:T(1,128)}, u32[]{:S(2)}) copy-start(f32[1,8192]{1,0:T(1,128)} %param.10) | copy-start | bytes 98308
  22.7 28.5 %copy-start.2 = (f32[128]{0:T(128)S(1)}, f32[128]{0:T(128)}, u32[]{:S(2)}) copy-start(f32[128]{0:T(128)} %param.15) | copy-start | bytes 1540
  47.2 7.7 copy-start.3
  52.9 104.7 %all-gather.7.cloned.1.call-start = ((), (), s32[]{:S(2)}) async-start(), calls=%async_computation | async-start | bytes 4456448 | tf_op jit(solution)/shard_map/all_gather | solution.py:9
  54.0 154.9 %all-gather.11.cloned.1.call-start = ((), (), s32[]{:S(2)}) async-start(), calls=%async_computation.2 | async-start | bytes 4456448 | tf_op jit(solution)/shard_map/all_gather | solution.py:9
  2088.0 3.6 copy-start
Sparse Core Ops, SparseCore 0:
  53.1 53.2 all-gather.8
  108.5 49.0 all-gather.6
  159.8 49.0 all-gather.10
where the time goes:
time: 2150 us; the launch traced here: 2140 us
  other arithmetic  1530 us (71%)
  matrix products  185 us (9%)
  local copies, waits for them, and re-layouts  123 us (6%)
  blocking collectives  101 us (5%)
  loops' own time  95.2 us (4%)
  waiting for transfers between devices  81.1 us (4%)
    another operation x119, other arithmetic, solve_parts(): factor_m = jnp.linalg.cholesky(middle)  590 us
    another operation x102, other arithmetic, solve_parts(): factor_c = jnp.linalg.cholesky(covar_a + (1.0 - live_a) * ident_state)  578 us
    another operation x51, other arithmetic, solve_parts(): jax.scipy.linalg.solve_triangular(factor_m, factor_c.T, lower=True)  335 us
    dot_general x161, matrix products, matmul(): jnp.dot(left, right, precision=lax.Precision.HIGHEST, preferred_element_t...  138 us
    another operation x1, loops' own time, entering(): return lax.fori_loop(0, count, lap, start)  94.2 us
    all_gather x3, waiting for transfers between devices, entering(): everything = jax.tree.map(lambda part: lax.all_gather(part, axis), array)  81 us
    another operation x166, local copies, waits for them, and re-layouts  72.6 us
  transfers between devices with their start and end apart: 3, of which 2 were waited for; matrix products, arithmetic and copies ran while one was open for 0% of the time, Pallas kernels for 0%

commit v1 on v0

v1 whole, which is shorter than its diff:
```python
import functools

import jax
import jax.numpy as jnp
from jax import lax
from jax.experimental import pallas as pl
from jax.experimental.pallas import tpu as pltpu
from jax.sharding import PartitionSpec as P

BF16 = jnp.bfloat16
F32 = jnp.float32
AXIS = "tm"
LANES = 128
PIECES = 8
LIMIT_FIRST = 1.0e-2
LIMIT_LATER = 1.5e-3


def gather_rounds(count):
    bits = count.bit_length() - 1
    rounds = []
    top = bits
    if bits > 1 and (bits - 1) % 2 == 1:
        rounds.append((bits - 1, 1))
        top = bits - 1
    while top > 1:
        rounds.append((top - 2, 2))
        top -= 2
    if bits > 0:
        rounds.append((0, 1))
    return rounds


def exchange(part, count):
    rows = part
    for shift, width in gather_rounds(count):
        pieces = [rows]
        for digit in range(1, 1 << width):
            flip = digit << shift
            pieces.append(lax.ppermute(rows, AXIS, [(p, p ^ flip) for p in range(count)]))
        rows = jnp.concatenate(pieces, axis=0)
    return rows


def slot_of(offset, count, local):
    slot = 0
    stride = local
    for shift, width in gather_rounds(count):
        slot = slot + ((offset >> shift) & ((1 << width) - 1)) * stride
        stride = stride << width
    return slot


def transition(mode_rate, mode_var):
    doubled = 2.0 * mode_rate
    damping = jnp.exp(-doubled)
    term_now = doubled * doubled * doubled / 6.0
    series = term_now
    for order in range(4, 15):
        term_now = term_now * doubled / order
        series = series + term_now
    q_value = mode_var * damping * series
    q_rate = mode_var * damping * (2.0 * doubled + series)
    q_cross = mode_var * damping * 2.0 * mode_rate * mode_rate
    root_value = jnp.sqrt(q_value)
    root_cross = q_cross / root_value
    root_rate = jnp.sqrt(q_value * q_rate - q_cross * q_cross) / root_value
    decay = jnp.exp(-mode_rate)
    return (
        decay * (1.0 + mode_rate),
        decay * mode_rate,
        -decay * mode_rate,
        decay * (1.0 - mode_rate),
        root_value,
        root_cross,
        root_rate,
        jnp.sqrt(mode_var),
    )


def split(x):
    high = x.astype(BF16)
    return high, (x - high.astype(F32)).astype(BF16)


def wide(x):
    return jnp.concatenate(split(x), axis=1)


def twice(x):
    return jnp.concatenate([x, x], axis=0)


def dot(left, right):
    return jnp.dot(left, right, preferred_element_type=F32)


def dot_split(left_wide, right_twice):
    both = dot(left_wide, right_twice)
    half = both.shape[1] // 2
    return both[:, :half] + both[:, half:]


def prepare_kernel(basis_ref, noise_ref, rate_ref, var_ref, scaled_t_ref, scaled_ref, root_ref, coef_ref):
    sensors, modes = basis_ref.shape
    root_ref[...] = lax.rsqrt(noise_ref[...])
    for start in range(0, sensors, LANES):
        span = slice(start, start + LANES)
        turned = basis_ref[span, :].T * root_ref[:, span]
        high, low = split(turned)
        scaled_t_ref[:modes, span] = high
        scaled_t_ref[modes:, span] = low
        scaled_ref[span, :] = wide(turned.T)
    f_vv, f_vr, f_rv, f_rr, root_value, root_cross, root_rate, sigma_vec = transition(rate_ref[...], var_ref[...])
    rows = (
        f_vv,
        f_vr,
        f_rv,
        f_rr,
        root_value * root_value,
        root_value * root_cross,
        root_cross * root_cross + root_rate * root_rate,
        sigma_vec * sigma_vec,
    )
    coef_ref[...] = jnp.concatenate(rows, axis=0)


def filter_kernel(
    position_ref,
    arrived_ref,
    block_ref,
    scaled_t_ref,
    scaled_ref,
    root_ref,
    noise_ref,
    coef_ref,
    field_ref,
    variances_ref,
    misfit_ref,
    bound_ref,
    p_vv,
    p_vr,
    p_rv,
    p_rr,
    pred_mean,
    columns,
    lam_now,
    mask_rows,
    readings,
    grads,
    means,
    diagonals,
    bounds,
    row_sums,
    *,
    count,
    local,
    blocks,
):
    modes = scaled_t_ref.shape[0] // 2
    sensors = scaled_t_ref.shape[1]
    steps = arrived_ref.shape[0]
    position = position_ref[0]
    row_index = lax.broadcasted_iota(jnp.int32, (modes, modes), 0)
    col_index = lax.broadcasted_iota(jnp.int32, (modes, modes), 1)
    eye = jnp.where(row_index == col_index, 1.0, 0.0).astype(F32)

    def coef(k):
        return coef_ref[k : k + 1, :]

    def slot(step):
        return slot_of((step // local) ^ position, count, local) + step % local

    def diagonal(square):
        return jnp.sum(eye * square, axis=0, keepdims=True)

    masks = arrived_ref[:, sensors : sensors + blocks].astype(BF16)
    block_index = lax.broadcasted_iota(jnp.int32, (blocks, sensors), 0)
    onehot = jnp.where(block_index == block_ref[...], 1.0, 0.0).astype(BF16)
    mask_rows[...] = dot(masks, onehot)
    readings[...] = mask_rows[...] * arrived_ref[:, :sensors] * root_ref[...]
    y_split = jnp.concatenate(split(readings[...]), axis=0)
    g_both = dot(y_split, scaled_ref[...])
    g_half = g_both[:, :modes] + g_both[:, modes:]
    grads[...] = g_half[:steps] + g_half[steps:]

    for k in range(4):
        columns[k] = jnp.broadcast_to(jnp.sum(eye * coef(k), axis=1, keepdims=True), (modes, modes))
    stationary = eye * coef(7)
    p_vv[...] = stationary
    p_rr[...] = stationary
    p_vr[...] = jnp.zeros((modes, modes), F32)
    p_rv[...] = jnp.zeros((modes, modes), F32)
    pred_mean[...] = jnp.zeros(pred_mean.shape, F32)
    bounds[...] = jnp.zeros(bounds.shape, F32)

    depth = sensors // PIECES

    def gram_piece(piece, at):
        span = slice(piece * depth, (piece + 1) * depth)
        left = scaled_t_ref[:modes, span] * mask_rows[pl.ds(at, 1), span].astype(BF16)
        return dot(left, scaled_ref[span, :])

    def gram_finish(total):
        cross = total[:, modes:]
        lam_now[...] = total[:, :modes] + cross + cross.T

    first = gram_piece(0, slot(0))
    for piece in range(1, PIECES):
        first = first + gram_piece(piece, slot(0))
    gram_finish(first)

    def one_step(step, carry):
        here = slot(step)
        ahead = slot(jnp.minimum(step + 1, steps - 1))
        lam = lam_now[...]
        pred_vv = p_vv[...]
        pred_rv = p_rv[...]
        pred_rr = p_rr[...]
        lam_wide = wide(lam)
        lam_p = dot_split(lam_wide, twice(wide(pred_vv)))
        cross = dot_split(lam_wide, twice(wide(p_vr[...])))
        total = gram_piece(0, ahead) + gram_piece(1, ahead)
        scale = 1.0 / (1.0 + diagonal(lam) * diagonal(pred_vv))
        rest = eye * (1.0 - scale) - lam_p * scale
        scaled_p = jnp.concatenate([pred_vv * scale, pred_rv * scale], axis=0)
        second = dot_split(wide(jnp.concatenate([rest, scaled_p], axis=0)), twice(wide(rest)))
        total = total + (gram_piece(2, ahead) + gram_piece(3, ahead))
        rest2 = second[:modes]
        cols1 = scaled_p + second[modes:]
        rest2_high = rest2.astype(BF16)
        cross_high, cross_low = split(cross)
        third = dot(
            jnp.concatenate([rest2_high, cols1.astype(BF16)], axis=0),
            jnp.concatenate([rest2_high, cross_high], axis=1),
        )
        total = total + (gram_piece(4, ahead) + gram_piece(5, ahead))
        rest4 = third[:modes, :modes]
        rest2_cross = third[:modes, modes:]
        cols_add = third[modes:, :modes]
        cols2 = cols1 + cols_add
        cols2_high, cols2_low = split(cols2)
        cols3 = cols2 + dot(cols2_high, rest4.astype(BF16))
        cross_wide = jnp.concatenate([cross_high, cross_low], axis=1)
        taken = dot_split(
            jnp.concatenate([cols2_high[modes:], cols2_low[modes:]], axis=1), twice(cross_wide)
        ) + dot(cols_add[modes:].astype(BF16), rest2_cross.astype(BF16))
        total = total + (gram_piece(6, ahead) + gram_piece(7, ahead))
        c_rr = pred_rr - taken
        c_vv = cols3[:modes]
        c_rv = cols3[modes:]
        c_vr = c_rv.T

        pull = grads[pl.ds(here, 1), :] - jnp.sum(lam * pred_mean[0], axis=0, keepdims=True)
        mean_v = pred_mean[0] + jnp.sum(c_vv * pull, axis=1, keepdims=True)
        mean_r = pred_mean[1] + jnp.sum(c_rv * pull, axis=1, keepdims=True)
        means[pl.ds(here, 1), :] = diagonal(mean_v)
        diagonals[pl.ds(here, 1), :] = jnp.concatenate([diagonal(c_vv), diagonal(c_rr)], axis=1)
        bounds[pl.ds(jnp.minimum(step, 1), 1), :] = jnp.maximum(
            bounds[pl.ds(jnp.minimum(step, 1), 1), :], jnp.sum(rest4 * rest4, axis=0, keepdims=True)
        )

        a, b, c, d = columns[0], columns[1], columns[2], columns[3]
        pred_mean[0] = a * mean_v + b * mean_r
        pred_mean[1] = c * mean_v + d * mean_r
        g_vv = a * c_vv + b * c_rv
        g_vr = a * c_vr + b * c_rr
        g_rv = c * c_vv + d * c_rv
        g_rr = c * c_vr + d * c_rr
        p_vv[...] = g_vv * coef(0) + g_vr * coef(1) + eye * coef(4)
        p_rv[...] = g_rv * coef(0) + g_rr * coef(1) + eye * coef(5)
        p_vr[...] = g_vv * coef(2) + g_vr * coef(3) + eye * coef(5)
        p_rr[...] = g_rv * coef(2) + g_rr * coef(3) + eye * coef(6)
        gram_finish(total)
        return carry

    lax.fori_loop(0, steps, one_step, 0)

    m_high, m_low = split(means[...])
    m_split = jnp.concatenate(
        [jnp.concatenate([m_high, m_high], axis=1), jnp.concatenate([m_low, m_low], axis=1)], axis=0
    )
    f_both = dot(m_split, scaled_t_ref[...])
    scaled_field = f_both[:steps] + f_both[steps:]
    field_ref[...] = scaled_field[:local] * (root_ref[...] * noise_ref[...])
    variances_ref[...] = diagonals[:local, :]
    gap = readings[...] - mask_rows[...] * scaled_field
    squares = gap * gap
    row_sums[...] = jnp.sum(squares.reshape(steps, sensors // LANES, LANES), axis=1)

    def add_row(step, total):
        return total + row_sums[pl.ds(slot(step), 1), :]

    lane_total = lax.fori_loop(0, steps, add_row, jnp.zeros((1, LANES), F32))
    misfit_ref[...] = jnp.sum(lane_total, axis=1, keepdims=True) / (steps * sensors)
    worst_first = jnp.sum(bounds[0:1], axis=1, keepdims=True) / (LIMIT_FIRST * LIMIT_FIRST)
    worst_later = jnp.sum(bounds[1:2], axis=1, keepdims=True) / (LIMIT_LATER * LIMIT_LATER)
    bound_ref[...] = jnp.maximum(worst_first, worst_later)


def matmul(left, right):
    return jnp.dot(left, right, precision=lax.Precision.HIGHEST, preferred_element_type=F32)


def careful(order, local, arrived, block_of_sensor, sensor_basis, noise_var, mode_rate, mode_var):
    sensors, modes = sensor_basis.shape
    blocks = arrived.shape[1] - sensors
    in_time = arrived[order]
    observations = in_time[:, :sensors]
    block_mask = in_time[:, sensors:]
    steps = observations.shape[0]
    f_vv, f_vr, f_rv, f_rr, root_value, root_cross, root_rate, sigma_vec = transition(mode_rate, mode_var)
    zero = jnp.zeros((modes, modes), F32)
    trans_mat = jnp.block([[jnp.diag(f_vv), jnp.diag(f_vr)], [jnp.diag(f_rv), jnp.diag(f_rr)]])
    lower_mat = jnp.block([[jnp.diag(root_value), zero], [jnp.diag(root_cross), jnp.diag(root_rate)]])
    noise_mat = matmul(lower_mat, lower_mat.T)
    stationary = jnp.diag(jnp.concatenate([sigma_vec * sigma_vec, sigma_vec * sigma_vec]))
    onehot = (block_of_sensor[:, None] == jnp.arange(blocks, dtype=jnp.int32)[None, :]).astype(F32)
    weights = matmul(block_mask, onehot.T) / noise_var[None, :]

    def one_step(carry, inputs):
        mean_vec, covar = carry
        weight_row, reading_row, step = inputs
        info_mat = matmul(sensor_basis.T * weight_row[None, :], sensor_basis)
        grad_vec = matmul((weight_row * reading_row)[None, :], sensor_basis)[0]
        trans_eff = jnp.where(step == 0, 0.0, trans_mat)
        noise_eff = jnp.where(step == 0, stationary, noise_mat)
        pred_mean = matmul(trans_eff, mean_vec[:, None])[:, 0]
        pred_cov = matmul(matmul(trans_eff, covar), trans_eff.T) + noise_eff
        factor_p = jnp.linalg.cholesky(pred_cov)
        top_rows = factor_p[:modes]
        inner = jnp.eye(2 * modes, dtype=F32) + matmul(matmul(top_rows.T, info_mat), top_rows)
        factor_m = jnp.linalg.cholesky(inner)
        solved = jax.scipy.linalg.solve_triangular(factor_m, factor_p.T, lower=True)
        new_cov = matmul(solved.T, solved)
        pull = grad_vec - matmul(info_mat, pred_mean[:modes, None])[:, 0]
        new_mean = pred_mean + matmul(new_cov[:, :modes], pull[:, None])[:, 0]
        return ((new_mean, new_cov), (new_mean, jnp.diagonal(new_cov)))

    start = (jnp.zeros((2 * modes,), F32), jnp.zeros((2 * modes, 2 * modes), F32))
    step_ids = jnp.arange(steps, dtype=jnp.int32)
    _, (means, variances) = lax.scan(one_step, start, (weights, observations, step_ids))
    field = matmul(means[:, :modes], sensor_basis.T)
    misfit = jnp.sum(weights * (observations - field) ** 2) / (steps * sensors)
    own = lax.axis_index(AXIS) * local
    own_field = lax.dynamic_slice_in_dim(field, own, local, 0)
    own_variances = lax.dynamic_slice_in_dim(variances, own, local, 0)
    return (own_field, own_variances, misfit.reshape(1, 1))


def in_vmem(count):
    return [pl.BlockSpec(memory_space=pltpu.VMEM)] * count


def on_device(observations, block_mask, block_of_sensor, sensor_basis, noise_var, mode_rate, mode_var):
    local, sensors = observations.shape
    modes = sensor_basis.shape[1]
    blocks = block_mask.shape[1]
    count = lax.axis_size(AXIS)
    steps = count * local
    noise_row = noise_var.reshape(1, sensors)
    position = lax.axis_index(AXIS).astype(jnp.int32)

    arrived = exchange(jnp.concatenate([observations, block_mask.astype(F32)], axis=1), count)

    scaled_t, scaled, root, coefs = pl.pallas_call(
        prepare_kernel,
        out_shape=(
            jax.ShapeDtypeStruct((2 * modes, sensors), BF16),
            jax.ShapeDtypeStruct((sensors, 2 * modes), BF16),
            jax.ShapeDtypeStruct((1, sensors), F32),
            jax.ShapeDtypeStruct((8, modes), F32),
        ),
        in_specs=in_vmem(4),
        out_specs=tuple(in_vmem(4)),
        compiler_params=pltpu.CompilerParams(vmem_limit_bytes=24 * 2**20),
        cost_estimate=pl.CostEstimate(flops=2 * sensors * modes, bytes_accessed=12 * sensors * modes, transcendentals=sensors),
        name="prepare",
    )(sensor_basis, noise_row, mode_rate.reshape(1, modes), mode_var.reshape(1, modes))

    square = pltpu.VMEM((modes, modes), F32)
    field, variances, misfit, bound = pl.pallas_call(
        functools.partial(filter_kernel, count=count, local=local, blocks=blocks),
        out_shape=(
            jax.ShapeDtypeStruct((local, sensors), F32),
            jax.ShapeDtypeStruct((local, 2 * modes), F32),
            jax.ShapeDtypeStruct((1, 1), F32),
            jax.ShapeDtypeStruct((1, 1), F32),
        ),
        in_specs=[pl.BlockSpec(memory_space=pltpu.SMEM)] + in_vmem(7),
        out_specs=tuple(in_vmem(4)),
        scratch_shapes=[
            square,
            square,
            square,
            square,
            pltpu.VMEM((2, modes, modes), F32),
            pltpu.VMEM((4, modes, modes), F32),
            square,
            pltpu.VMEM((steps, sensors), F32),
            pltpu.VMEM((steps, sensors), F32),
            pltpu.VMEM((steps, modes), F32),
            pltpu.VMEM((steps, modes), F32),
            pltpu.VMEM((steps, 2 * modes), F32),
            pltpu.VMEM((8, modes), F32),
            pltpu.VMEM((steps, LANES), F32),
        ],
        compiler_params=pltpu.CompilerParams(vmem_limit_bytes=40 * 2**20),
        cost_estimate=pl.CostEstimate(flops=steps * sensors * modes * 512, bytes_accessed=8 * sensors * modes, transcendentals=0),
        name="filter",
    )(position.reshape(1), arrived, block_of_sensor.reshape(1, sensors), scaled_t, scaled, root, noise_row, coefs)

    step_ids = jnp.arange(steps, dtype=jnp.int32)
    order = slot_of((step_ids // local) ^ position, count, local) + step_ids % local
    field, variances, misfit = lax.cond(
        bound[0, 0] <= 1.0,
        lambda: (field, variances, misfit),
        lambda: careful(order, local, arrived, block_of_sensor, sensor_basis, noise_var, mode_rate, mode_var),
    )
    return (field, variances, misfit.reshape(1))


def solution(mesh):
    in_specs = (P(("groups", "tm"), None), P(("groups", "tm"), None), P(), P(), P(), P(), P())
    out_specs = (P(("groups", "tm"), None), P(("groups", "tm"), None), P("groups"))
    return jax.shard_map(on_device, mesh=mesh, in_specs=in_specs, out_specs=out_specs, check_vma=False)
```

time: 2150 us -> 57.9 us (0.03)
  other arithmetic: 1530 us -> 2.28 us
  matrix products: 185 us -> 0 us
  local copies, waits for them, and re-layouts: 123 us -> 11.5 us
  blocking collectives: 101 us -> 0 us
  loops' own time: 95.2 us -> 0.88 us
  waiting for transfers between devices: 81.1 us -> 5.69 us
  Pallas kernels: 0 us -> 25.5 us
    another operation x277 -> x0, other arithmetic: 1530 us -> none  [the longest x119 590 us: solve_parts(): factor_m = jnp.linalg.cholesky(middle)]
    dot_general x162 -> x0, matrix products: 150 us -> none  [the longest x161 138 us: matmul(): jnp.dot(left, right, precision=lax.Precision.HIGHEST, preferred_element_t...]
    another operation x18 -> x1, loops' own time: 95.2 us -> 0.88 us  [on_device(): lax.cond(bound[0, 0] <= 1.0, lambda: (field, variances, misfit), lambda:...]
    another operation x354 -> x0, local copies, waits for them, and re-layouts: 81.3 us -> none
    all_gather x3 -> x0, waiting for transfers between devices: 81 us -> none  [entering(): everything = jax.tree.map(lambda part: lax.all_gather(part, axis), array)]
    all_gather x2 -> x0, blocking collectives: 40.5 us -> none  [entering(): everything = jax.tree.map(lambda part: lax.all_gather(part, axis), array)]
    another operation x120 -> x0, matrix products: 35.3 us -> none  [the longest x51 15.7 us: solve_parts(): jax.scipy.linalg.solve_triangular(factor_m, factor_c.T, lower=True)]
    unnamed x1 -> x0, blocking collectives: 31 us -> none
  transfers between devices with their start and end apart: 3 -> 5, of which waited for: 2 -> 4; matrix products, arithmetic and copies ran while one was open for 0% -> 0% of each run, Pallas kernels for 0% -> 8%
where the time goes in v1:
time: 57.9 us; the launch traced here: 57.5 us
  Pallas kernels  25.5 us (44%)
  local copies, waits for them, and re-layouts  11.5 us (20%)
  starting transfers between devices  9.1 us (16%)
  waiting for transfers between devices  5.69 us (10%)
  between operations  2.57 us (4%)
  other arithmetic  2.28 us (4%)
  loops' own time  0.88 us (2%)
    pallas_call x1, Pallas kernels, on_device(): pl.pallas_call(functools.partial(filter_kernel, count=count, local=local,...  21 us
    ppermute x5, starting transfers between devices, exchange(): lax.ppermute(rows, AXIS, [(p, p ^ flip) for p in range(count)])  9.1 us
    unnamed x16, local copies, waits for them, and re-layouts  8.29 us
    ppermute x5, waiting for transfers between devices, exchange(): lax.ppermute(rows, AXIS, [(p, p ^ flip) for p in range(count)])  5.69 us
    pallas_call x1, Pallas kernels, on_device(): pl.pallas_call(prepare_kernel, out_shape=(jax.ShapeDtypeStruct((2 * modes...  4.54 us
    concatenate x2, local copies, waits for them, and re-layouts, exchange(): rows = jnp.concatenate(pieces, axis=0)  3.18 us
  transfers between devices with their start and end apart: 5, of which 4 were waited for; matrix products, arithmetic and copies ran while one was open for 0% of the time, Pallas kernels for 8%

profile of v1, /device:TPU:1, one launch (start us, length us, event | category | flops | bytes accessed | tf_op | source)
XLA Modules:
  0.0 57.5 jit_solution(17554743325174467555)
XLA Ops:
  0.6 0.0 copy-start.4
  0.6 0.0 copy-start.7
  0.7 0.7 %convert_element_type.13 = f32[1,64]{1,0:T(1,128)S(1)} convert(s32[1,64]{1,0:T(1,128)} %param.13) | non-fusion elementwise | flops 64 | bytes 512 | tf_op jit(solution)/shard_map/convert_element_type | solution.py:364
  1.3 0.8 %pad_maximum_fusion.2 = f32[1,8256]{1,0:T(1,128)S(1)} fusion(f32[1,64]{1,0:T(1,128)S(1)} %convert_element_type.13, f32[1,8192]{1,0:T(1,128)} %param.12), kind=kLoop, calls=%fused_computation.139 | loop fusion | flops 8256 | bytes 66048 | tf_op jit(solution)/shard_map/concatenate | solution.py:364
  2.1 3.2 %collective-permute-start = (f32[1,8256]{1,0:T(1,128)S(1)}, f32[1,8256]{1,0:T(1,128)S(1)}, u32[]{:S(2)}, u32[]{:S(2)}) collective-permute-start(f32[1,8256]{1,0:T(1,128)S(1)} %pad_maximum_fusion.2), channel_id=1, source_target_pairs={{0,8},{1,9},{2,10},{3,11},{4,12},{5,13},{6,14},{7,15},{8,0},{9,1},... | collective-permute-start | bytes 99080 | tf_op jit(solution)/shard_map/ppermute | solution.py:40
  5.3 1.3 %collective-permute-done = f32[1,8256]{1,0:T(1,128)S(1)} collective-permute-done((f32[1,8256]{1,0:T(1,128)S(1)}, f32[1,8256]{1,0:T(1,128)S(1)}, u32[]{:S(2)}, u32[]{:S(2)}) %collective-permute-start) | collective-permute-done | bytes 33056 | tf_op jit(solution)/shard_map/ppermute | solution.py:40
  6.6 0.8 %pad_maximum_fusion.1 = f32[2,8256]{1,0:T(2,128)S(1)} fusion(f32[1,8256]{1,0:T(1,128)S(1)} %collective-permute-done, f32[1,64]{1,0:T(1,128)S(1)} %convert_element_type.13, f32[1,8192]{1,0:T(1,128)} %param.12), kind=kLoop, calls=%fused_computation.138 | loop fusion | flops 33024 | bytes 132096 | tf_op jit(solution)/shard_map/concatenate | solution.py:41
  7.5 1.4 %collective-permute-start.1 = (f32[2,8256]{1,0:T(2,128)S(1)}, f32[2,8256]{1,0:T(2,128)S(1)}, u32[]{:S(2)}, u32[]{:S(2)}) collective-permute-start(f32[2,8256]{1,0:T(2,128)S(1)} %pad_maximum_fusion.1), channel_id=1, source_target_pairs={{0,2},{1,3},{2,0},{3,1},{4,6},{5,7},{6,4},{7,5},{8,10},{9,11},{10,... | collective-permute-start | bytes 198152 | tf_op jit(solution)/shard_map/ppermute | solution.py:40
  8.8 1.3 %collective-permute-start.2 = (f32[2,8256]{1,0:T(2,128)S(1)}, f32[2,8256]{1,0:T(2,128)S(1)}, u32[]{:S(2)}, u32[]{:S(2)}) collective-permute-start(f32[2,8256]{1,0:T(2,128)S(1)} %pad_maximum_fusion.1), channel_id=1, source_target_pairs={{0,4},{1,5},{2,6},{3,7},{4,0},{5,1},{6,2},{7,3},{8,12},{9,13},{10,... | collective-permute-start | bytes 198152 | tf_op jit(solution)/shard_map/ppermute | solution.py:40
  10.1 0.0 collective-permute-start.3
  10.2 0.5 collective-permute-done.1
  10.6 1.3 %collective-permute-done.2 = f32[2,8256]{1,0:T(2,128)S(1)} collective-permute-done((f32[2,8256]{1,0:T(2,128)S(1)}, f32[2,8256]{1,0:T(2,128)S(1)}, u32[]{:S(2)}, u32[]{:S(2)}) %collective-permute-start.2) | collective-permute-done | bytes 66080 | tf_op jit(solution)/shard_map/ppermute | solution.py:40
  11.9 2.6 %collective-permute-done.3 = f32[2,8256]{1,0:T(2,128)S(1)} collective-permute-done((f32[2,8256]{1,0:T(2,128)S(1)}, f32[2,8256]{1,0:T(2,128)S(1)}, u32[]{:S(2)}, u32[]{:S(2)}) %collective-permute-start.3) | collective-permute-done | bytes 66080 | tf_op jit(solution)/shard_map/ppermute | solution.py:40
  14.5 1.2 %concatenate.59 = f32[8,8256]{1,0:T(8,128)S(1)} concatenate(f32[1,8256]{1,0:T(1,128)S(1)} %pad_maximum_fusion.2, f32[1,8256]{1,0:T(1,128)S(1)} %collective-permute-done, f32[2,8256]{1,0:T(2,128)S(1)} %collective-permute-done.1, f32[2,8256]{1,0:T(2,128)S(1)} %collective-permute-done.2, f32[2,8256]{1,0:T(2,128)S(1)} %collective-permute-done.3), dimensions={0} | concatenate | bytes 528384 | tf_op jit(solution)/shard_map/concatenate | solution.py:41
  15.7 3.2 %collective-permute-start.4 = (f32[8,8256]{1,0:T(8,128)S(1)}, f32[8,8256]{1,0:T(8,128)S(1)}, u32[]{:S(2)}, u32[]{:S(2)}) collective-permute-start(f32[8,8256]{1,0:T(8,128)S(1)} %concatenate.59), channel_id=1, source_target_pairs={{0,1},{1,0},{2,3},{3,2},{4,5},{5,4},{6,7},{7,6},{8,9},{9,8},{10,11... | collective-permute-start | bytes 792584 | tf_op jit(solution)/shard_map/ppermute | solution.py:40
  18.9 4.5 %prepare.1 = (bf16[256,8192]{1,0:T(8,128)(2,1)S(1)}, bf16[8192,256]{1,0:T(8,128)(2,1)S(1)}, f32[1,8192]{1,0:T(1,128)S(1)}, f32[8,128]{1,0:T(8,128)S(1)}) custom-call(f32[8192,128]{1,0:T(8,128)} %basis_ref.1, f32[1,8192]{1,0:T(1,128)} %bitcast.167, f32[1,128]{1,0:T(1,128)} %bitcast.169, f32[1,128]{1,0:T(1,128)} %bitcast.170), custom_call_target="tpu_custom_call" | custom-call | flops 2097152 | bytes 12582912 | tf_op jit(solution)/shard_map/prepare/pallas_call | solution.py:366
  23.4 0.0 copy-start
  23.4 1.9 %copy-done = bf16[256,8192]{1,0:T(8,128)(2,1)} copy-done((bf16[256,8192]{1,0:T(8,128)(2,1)}, bf16[256,8192]{1,0:T(8,128)(2,1)S(1)}, u32[]{:S(2)}) %copy-start) | copy-done | bytes 4194328
  25.4 0.0 copy-start.2
  25.4 2.0 %copy-done.2 = bf16[8192,256]{1,0:T(8,128)(2,1)} copy-done((bf16[8192,256]{1,0:T(8,128)(2,1)}, bf16[8192,256]{1,0:T(8,128)(2,1)S(1)}, u32[]{:S(2)}) %copy-start.2) | copy-done | bytes 4194328
  27.4 0.0 collective-permute-done.4
  27.4 2.0 %concatenate.60.arrived_ref = f32[16,8256]{1,0:T(8,128)S(1)} concatenate(f32[1,8256]{1,0:T(1,128)S(1)} %pad_maximum_fusion.2, f32[1,8256]{1,0:T(1,128)S(1)} %collective-permute-done, f32[2,8256]{1,0:T(2,128)S(1)} %collective-permute-done.1, f32[2,8256]{1,0:T(2,128)S(1)} %collective-permute-done.2, f32[2,8256]{1,0:T(2,128)S(1)} %collective-permute-done.3, ...), dimensions={0} | concatenate | bytes 1056768 | tf_op jit(solution)/shard_map/concatenate | solution.py:41
  29.4 0.0 copy-done.4
  29.4 0.0 copy-done.7
  29.4 0.0 copy-start.1
  29.4 2.2 %copy-done.1 = bf16[256,8192]{1,0:T(8,128)(2,1)S(1)} copy-done((bf16[256,8192]{1,0:T(8,128)(2,1)S(1)}, bf16[256,8192]{1,0:T(8,128)(2,1)}, u32[]{:S(2)}) %copy-start.1) | copy-done | bytes 4194328
  31.6 0.0 copy-start.3
  31.6 2.2 %copy-done.3 = bf16[8192,256]{1,0:T(8,128)(2,1)S(1)} copy-done((bf16[8192,256]{1,0:T(8,128)(2,1)S(1)}, bf16[8192,256]{1,0:T(8,128)(2,1)}, u32[]{:S(2)}) %copy-start.3) | copy-done | bytes 4194328
  33.8 0.0 copy-start.5
  33.8 0.0 copy-start.6
  33.8 21.0 %filter.1 = (f32[1,8192]{1,0:T(1,128)}, f32[1,256]{1,0:T(1,128)}, f32[1,1]{1,0:T(1,128)}, f32[1,1]{1,0:T(1,128)}) custom-call(s32[1]{0:T(128)} %bitcast.2.position_ref, f32[16,8256]{1,0:T(8,128)S(1)} %concatenate.60.arrived_ref, s32[1,8192]{1,0:T(1,128)S(1)} %bitcast.171, bf16[256,8192]{1,0:T(8,128)(2,1)S(1)} %copy-done.1, bf16[8192,256]{1,0:T(8,128)(2,1)S(1)} %copy-done.3, ...), custom_call_target="tpu_custom_call" | custom-call | flops 8589934592 | bytes 8388608 | tf_op jit(solution)/shard_map/filter/pallas_call | solution.py:382
  55.5 0.0 copy-done.5
  55.5 0.0 copy-done.6
  55.5 0.9 %conditional.1 = (f32[1,8192]{1,0:T(1,128)}, f32[1,256]{1,0:T(1,128)}, f32[1]{0:T(128)}) conditional(s32[]{:T(128)} %bitcast.7, (s32[]{:T(128)}, s32[16]{0:T(128)S(1)}, f32[16,8256]{1,0:T(8,128)S(1)}, s32[8192]{0:T(1024)S(1)}, f32[8192]{0:T(1024)S(1)}, /*index=5*/f32[128]{0:T(128)S(1)}, f32[128]{0:T(128)S(1)}, f32[8192,128]{1,0:T(8,128)}) %tuple.122, ...), branch_computations={%region_0.9_spmd, %region_8.10_spmd} | conditional | flops 3139375104 | bytes 30772696 | solution.py:415
  (1 shorter events, 0.0 us)
Async XLA Ops:
  0.6 28.8 %copy-start.4 = (f32[8192]{0:T(1024)S(1)}, f32[8192]{0:T(1024)}, u32[]{:S(2)}) copy-start(f32[8192]{0:T(1024)} %param.16) | copy-start | bytes 98308
  0.6 28.8 %copy-start.7 = (s32[8192]{0:T(1024)S(1)}, s32[8192]{0:T(1024)}, u32[]{:S(2)}) copy-start(s32[8192]{0:T(1024)} %param.14) | copy-start | bytes 98308
  2.1 4.5 %collective-permute-start = (f32[1,8256]{1,0:T(1,128)S(1)}, f32[1,8256]{1,0:T(1,128)S(1)}, u32[]{:S(2)}, u32[]{:S(2)}) collective-permute-start(f32[1,8256]{1,0:T(1,128)S(1)} %pad_maximum_fusion.2), channel_id=1, source_target_pairs={{0,8},{1,9},{2,10},{3,11},{4,12},{5,13},{6,14},{7,15},{8,0},{9,1},... | collective-permute-start | bytes 99080 | tf_op jit(solution)/shard_map/ppermute | solution.py:40
  7.5 3.2 %collective-permute-start.1 = (f32[2,8256]{1,0:T(2,128)S(1)}, f32[2,8256]{1,0:T(2,128)S(1)}, u32[]{:S(2)}, u32[]{:S(2)}) collective-permute-start(f32[2,8256]{1,0:T(2,128)S(1)} %pad_maximum_fusion.1), channel_id=1, source_target_pairs={{0,2},{1,3},{2,0},{3,1},{4,6},{5,7},{6,4},{7,5},{8,10},{9,11},{10,... | collective-permute-start | bytes 198152 | tf_op jit(solution)/shard_map/ppermute | solution.py:40
  8.8 3.1 %collective-permute-start.2 = (f32[2,8256]{1,0:T(2,128)S(1)}, f32[2,8256]{1,0:T(2,128)S(1)}, u32[]{:S(2)}, u32[]{:S(2)}) collective-permute-start(f32[2,8256]{1,0:T(2,128)S(1)} %pad_maximum_fusion.1), channel_id=1, source_target_pairs={{0,4},{1,5},{2,6},{3,7},{4,0},{5,1},{6,2},{7,3},{8,12},{9,13},{10,... | collective-permute-start | bytes 198152 | tf_op jit(solution)/shard_map/ppermute | solution.py:40
  10.1 4.4 %collective-permute-start.3 = (f32[2,8256]{1,0:T(2,128)S(1)}, f32[2,8256]{1,0:T(2,128)S(1)}, u32[]{:S(2)}, u32[]{:S(2)}) collective-permute-start(f32[2,8256]{1,0:T(2,128)S(1)} %pad_maximum_fusion.1), channel_id=1, source_target_pairs={{0,6},{1,7},{2,4},{3,5},{4,2},{5,3},{6,0},{7,1},{8,14},{9,15},{10,... | collective-permute-start | bytes 198152 | tf_op jit(solution)/shard_map/ppermute | solution.py:40
  15.7 11.6 %collective-permute-start.4 = (f32[8,8256]{1,0:T(8,128)S(1)}, f32[8,8256]{1,0:T(8,128)S(1)}, u32[]{:S(2)}, u32[]{:S(2)}) collective-permute-start(f32[8,8256]{1,0:T(8,128)S(1)} %concatenate.59), channel_id=1, source_target_pairs={{0,1},{1,0},{2,3},{3,2},{4,5},{5,4},{6,7},{7,6},{8,9},{9,8},{10,11... | collective-permute-start | bytes 792584 | tf_op jit(solution)/shard_map/ppermute | solution.py:40
  23.4 1.9 %copy-start = (bf16[256,8192]{1,0:T(8,128)(2,1)}, bf16[256,8192]{1,0:T(8,128)(2,1)S(1)}, u32[]{:S(2)}) copy-start(bf16[256,8192]{1,0:T(8,128)(2,1)S(1)} %get-tuple-element.180.scaled_t_ref) | copy-start | bytes 12582916
  25.4 2.0 %copy-start.2 = (bf16[8192,256]{1,0:T(8,128)(2,1)}, bf16[8192,256]{1,0:T(8,128)(2,1)S(1)}, u32[]{:S(2)}) copy-start(bf16[8192,256]{1,0:T(8,128)(2,1)S(1)} %get-tuple-element.181.scaled_ref) | copy-start | bytes 12582916
  29.4 2.2 %copy-start.1 = (bf16[256,8192]{1,0:T(8,128)(2,1)S(1)}, bf16[256,8192]{1,0:T(8,128)(2,1)}, u32[]{:S(2)}) copy-start(bf16[256,8192]{1,0:T(8,128)(2,1)} %copy-done) | copy-start | bytes 12582916
  31.6 2.2 %copy-start.3 = (bf16[8192,256]{1,0:T(8,128)(2,1)S(1)}, bf16[8192,256]{1,0:T(8,128)(2,1)}, u32[]{:S(2)}) copy-start(bf16[8192,256]{1,0:T(8,128)(2,1)} %copy-done.2) | copy-start | bytes 12582916
  33.8 21.7 %copy-start.5 = (f32[128]{0:T(128)S(1)}, f32[128]{0:T(128)}, u32[]{:S(2)}) copy-start(f32[128]{0:T(128)} %param.17) | copy-start | bytes 1540
  33.8 21.7 %copy-start.6 = (f32[128]{0:T(128)S(1)}, f32[128]{0:T(128)}, u32[]{:S(2)}) copy-start(f32[128]{0:T(128)} %param.18) | copy-start | bytes 1540

commit v2 on v1

--- a/solution.py
+++ b/solution.py
@@ -12,6 +12,7 @@
 AXIS = "tm"
 LANES = 128
 PIECES = 8
+COPIES = 8
 LIMIT_FIRST = 1.0e-2
 LIMIT_LATER = 1.5e-3
 
@@ -31,15 +32,35 @@
     return rounds
 
 
-def exchange(part, count):
-    rows = part
-    for shift, width in gather_rounds(count):
-        pieces = [rows]
-        for digit in range(1, 1 << width):
-            flip = digit << shift
-            pieces.append(lax.ppermute(rows, AXIS, [(p, p ^ flip) for p in range(count)]))
-        rows = jnp.concatenate(pieces, axis=0)
-    return rows
+def swap(array, flip, count):
+    return lax.ppermute(array, AXIS, [(p, p ^ flip) for p in range(count)])
+
+
+def pack(observations, block_mask):
+    local, sensors = observations.shape
+    mask_row = jnp.pad(block_mask.astype(F32), ((0, 0), (0, LANES - block_mask.shape[1])))
+    mask_tile = jnp.pad(mask_row.reshape(local, 1, LANES), ((0, 0), (0, 7), (0, 0)))
+    return jnp.concatenate([observations.reshape(local, sensors // LANES, LANES), mask_tile], axis=1)
+
+
+def exchange(observations, block_mask, count, early, late, seed):
+    rounds = gather_rounds(count)
+    pieces = [pack(observations, block_mask)]
+    done = None
+    for turn, (shift, width) in enumerate(rounds):
+        flips = [digit << shift for digit in range(1, 1 << width)]
+        rows = pieces[0] if turn == 0 else jnp.concatenate(pieces, axis=0)
+        if turn == len(rounds) - 2:
+            rows, seed = lax.optimization_barrier((rows, seed))
+            seed = early(seed)
+        if turn == len(rounds) - 1:
+            rows, seed = lax.optimization_barrier((rows, seed))
+            done = late(seed)
+        if turn == 0:
+            pieces = [rows] + [pack(swap(observations, flip, count), swap(block_mask, flip, count)) for flip in flips]
+        else:
+            pieces = [rows] + [swap(rows, flip, count) for flip in flips]
+    return pieces, done
 
 
 def slot_of(offset, count, local):
@@ -101,16 +122,30 @@
     return both[:, :half] + both[:, half:]
 
 
-def prepare_kernel(basis_ref, noise_ref, rate_ref, var_ref, scaled_t_ref, scaled_ref, root_ref, coef_ref):
+def dot_three(left_wide, right):
+    high, low = split(right)
+    return dot(left_wide, twice(high)) + dot(left_wide[:, : high.shape[0]], low)
+
+
+def prepare_kernel(
+    basis_ref,
+    block_ref,
+    rate_ref,
+    var_ref,
+    scaled_t_ref,
+    scaled_ref,
+    onehot_ref,
+    coef_ref,
+    basis,
+    arrivals,
+):
     sensors, modes = basis_ref.shape
-    root_ref[...] = lax.rsqrt(noise_ref[...])
-    for start in range(0, sensors, LANES):
-        span = slice(start, start + LANES)
-        turned = basis_ref[span, :].T * root_ref[:, span]
-        high, low = split(turned)
-        scaled_t_ref[:modes, span] = high
-        scaled_t_ref[modes:, span] = low
-        scaled_ref[span, :] = wide(turned.T)
+    depth = sensors // COPIES
+    copies = []
+    for part in range(COPIES):
+        rows = pl.ds(part * depth, depth)
+        copies.append(pltpu.make_async_copy(basis_ref.at[rows], basis.at[rows], arrivals.at[part]))
+        copies[part].start()
     f_vv, f_vr, f_rv, f_rr, root_value, root_cross, root_rate, sigma_vec = transition(rate_ref[...], var_ref[...])
     rows = (
         f_vv,
@@ -123,43 +158,52 @@
         sigma_vec * sigma_vec,
     )
     coef_ref[...] = jnp.concatenate(rows, axis=0)
-
-
-def filter_kernel(
-    position_ref,
-    arrived_ref,
-    block_ref,
-    scaled_t_ref,
-    scaled_ref,
-    root_ref,
-    noise_ref,
-    coef_ref,
-    field_ref,
-    variances_ref,
-    misfit_ref,
-    bound_ref,
-    p_vv,
-    p_vr,
-    p_rv,
-    p_rr,
-    pred_mean,
-    columns,
-    lam_now,
-    mask_rows,
-    readings,
-    grads,
-    means,
-    diagonals,
-    bounds,
-    row_sums,
-    *,
-    count,
-    local,
-    blocks,
-):
+    block_index = lax.broadcasted_iota(jnp.int32, onehot_ref.shape, 0)
+    onehot_ref[...] = jnp.where(block_index == block_ref[...], 1.0, 0.0).astype(BF16)
+    for start in range(0, sensors, LANES):
+        if start % depth == 0:
+            copies[start // depth].wait()
+        span = slice(start, start + LANES)
+        chunk = basis[span, :]
+        high, low = split(chunk.T)
+        scaled_t_ref[:modes, span] = high
+        scaled_t_ref[modes:, span] = low
+        scaled_ref[span, :] = wide(chunk)
+
+
+def filter_kernel(position_ref, *refs, count, local, blocks, parts):
+    pieces = refs[:parts]
+    (
+        onehot_ref,
+        scaled_t_ref,
+        scaled_ref,
+        noise_ref,
+        coef_ref,
+        field_ref,
+        variances_ref,
+        misfit_ref,
+        bound_ref,
+        p_vv,
+        p_vr,
+        p_rv,
+        p_rr,
+        pred_mean,
+        columns,
+        lam_now,
+        root_ref,
+        mask_rows,
+        readings,
+        grads,
+        means,
+        diagonals,
+        bounds,
+        row_sums,
+    ) = refs[parts:]
     modes = scaled_t_ref.shape[0] // 2
     sensors = scaled_t_ref.shape[1]
-    steps = arrived_ref.shape[0]
+    piece_rows = pieces[0].shape[0]
+    steps = parts * piece_rows
+    chunks = sensors // LANES
     position = position_ref[0]
     row_index = lax.broadcasted_iota(jnp.int32, (modes, modes), 0)
     col_index = lax.broadcasted_iota(jnp.int32, (modes, modes), 1)
@@ -174,16 +218,13 @@
     def diagonal(square):
         return jnp.sum(eye * square, axis=0, keepdims=True)
 
-    masks = arrived_ref[:, sensors : sensors + blocks].astype(BF16)
-    block_index = lax.broadcasted_iota(jnp.int32, (blocks, sensors), 0)
-    onehot = jnp.where(block_index == block_ref[...], 1.0, 0.0).astype(BF16)
-    mask_rows[...] = dot(masks, onehot)
-    readings[...] = mask_rows[...] * arrived_ref[:, :sensors] * root_ref[...]
-    y_split = jnp.concatenate(split(readings[...]), axis=0)
-    g_both = dot(y_split, scaled_ref[...])
-    g_half = g_both[:, :modes] + g_both[:, modes:]
-    grads[...] = g_half[:steps] + g_half[steps:]
-
+    root_ref[...] = lax.rsqrt(noise_ref[...])
+    masks = jnp.concatenate([ref[:, chunks, :blocks] for ref in pieces], axis=0).astype(BF16)
+    mask_rows[...] = dot(masks, onehot_ref[...])
+    for chunk in range(chunks):
+        span = slice(chunk * LANES, (chunk + 1) * LANES)
+        rows = jnp.concatenate([ref[:, chunk, :] for ref in pieces], axis=0)
+        readings[:, span] = mask_rows[:, span] * rows * root_ref[:, span]
     for k in range(4):
         columns[k] = jnp.broadcast_to(jnp.sum(eye * coef(k), axis=1, keepdims=True), (modes, modes))
     stationary = eye * coef(7)
@@ -205,10 +246,12 @@
         cross = total[:, modes:]
         lam_now[...] = total[:, :modes] + cross + cross.T
 
-    first = gram_piece(0, slot(0))
-    for piece in range(1, PIECES):
-        first = first + gram_piece(piece, slot(0))
-    gram_finish(first)
+    first_left = scaled_t_ref[:modes, :] * mask_rows[pl.ds(slot(0), 1), :].astype(BF16)
+    y_high, y_low = split(readings[...])
+    first = dot(jnp.concatenate([first_left, y_high, y_low], axis=0), scaled_ref[...])
+    gram_finish(first[:modes])
+    g_half = first[modes:, :modes] + first[modes:, modes:]
+    grads[...] = g_half[:steps] + g_half[steps:]
 
     def one_step(step, carry):
         here = slot(step)
@@ -218,8 +261,8 @@
         pred_rv = p_rv[...]
         pred_rr = p_rr[...]
         lam_wide = wide(lam)
-        lam_p = dot_split(lam_wide, twice(wide(pred_vv)))
-        cross = dot_split(lam_wide, twice(wide(p_vr[...])))
+        lam_p = dot_three(lam_wide, pred_vv)
+        cross = dot_three(lam_wide, p_vr[...])
         total = gram_piece(0, ahead) + gram_piece(1, ahead)
         scale = 1.0 / (1.0 + diagonal(lam) * diagonal(pred_vv))
         rest = eye * (1.0 - scale) - lam_p * scale
@@ -230,17 +273,13 @@
         cols1 = scaled_p + second[modes:]
         rest2_high = rest2.astype(BF16)
         cross_high, cross_low = split(cross)
-        third = dot(
-            jnp.concatenate([rest2_high, cols1.astype(BF16)], axis=0),
-            jnp.concatenate([rest2_high, cross_high], axis=1),
-        )
+        rest4 = dot(rest2_high, rest2_high).astype(BF16)
+        rest2_cross = dot(rest2_high, cross_high)
+        cols_add = dot(cols1.astype(BF16), rest2_high)
         total = total + (gram_piece(4, ahead) + gram_piece(5, ahead))
-        rest4 = third[:modes, :modes]
-        rest2_cross = third[:modes, modes:]
-        cols_add = third[modes:, :modes]
         cols2 = cols1 + cols_add
         cols2_high, cols2_low = split(cols2)
-        cols3 = cols2 + dot(cols2_high, rest4.astype(BF16))
+        cols3 = cols2 + dot(cols2_high, rest4)
         cross_wide = jnp.concatenate([cross_high, cross_low], axis=1)
         taken = dot_split(
             jnp.concatenate([cols2_high[modes:], cols2_low[modes:]], axis=1), twice(cross_wide)
@@ -249,15 +288,18 @@
         c_rr = pred_rr - taken
         c_vv = cols3[:modes]
         c_rv = cols3[modes:]
-        c_vr = c_rv.T
+        c_vr = cols2[modes:].T + lax.dot_general(
+            rest4, cols2_high[modes:], (((0,), (1,)), ((), ())), preferred_element_type=F32
+        )
 
         pull = grads[pl.ds(here, 1), :] - jnp.sum(lam * pred_mean[0], axis=0, keepdims=True)
         mean_v = pred_mean[0] + jnp.sum(c_vv * pull, axis=1, keepdims=True)
         mean_r = pred_mean[1] + jnp.sum(c_rv * pull, axis=1, keepdims=True)
         means[pl.ds(here, 1), :] = diagonal(mean_v)
         diagonals[pl.ds(here, 1), :] = jnp.concatenate([diagonal(c_vv), diagonal(c_rr)], axis=1)
+        rest4_f32 = rest4.astype(F32)
         bounds[pl.ds(jnp.minimum(step, 1), 1), :] = jnp.maximum(
-            bounds[pl.ds(jnp.minimum(step, 1), 1), :], jnp.sum(rest4 * rest4, axis=0, keepdims=True)
+            bounds[pl.ds(jnp.minimum(step, 1), 1), :], jnp.sum(rest4_f32 * rest4_f32, axis=0, keepdims=True)
         )
 
         a, b, c, d = columns[0], columns[1], columns[2], columns[3]
@@ -302,12 +344,12 @@
     return jnp.dot(left, right, precision=lax.Precision.HIGHEST, preferred_element_type=F32)
 
 
-def careful(order, local, arrived, block_of_sensor, sensor_basis, noise_var, mode_rate, mode_var):
+def careful(order, local, blocks, arrived, block_of_sensor, sensor_basis, noise_var, mode_rate, mode_var):
     sensors, modes = sensor_basis.shape
-    blocks = arrived.shape[1] - sensors
+    chunks = sensors // LANES
     in_time = arrived[order]
-    observations = in_time[:, :sensors]
-    block_mask = in_time[:, sensors:]
+    observations = in_time[:, :chunks, :].reshape(-1, sensors)
+    block_mask = in_time[:, chunks, :blocks]
     steps = observations.shape[0]
     f_vv, f_vr, f_rv, f_rr, root_value, root_cross, root_rate, sigma_vec = transition(mode_rate, mode_var)
     zero = jnp.zeros((modes, modes), F32)
@@ -361,33 +403,45 @@
     noise_row = noise_var.reshape(1, sensors)
     position = lax.axis_index(AXIS).astype(jnp.int32)
 
-    arrived = exchange(jnp.concatenate([observations, block_mask.astype(F32)], axis=1), count)
-
-    scaled_t, scaled, root, coefs = pl.pallas_call(
+    prepare = pl.pallas_call(
         prepare_kernel,
         out_shape=(
             jax.ShapeDtypeStruct((2 * modes, sensors), BF16),
             jax.ShapeDtypeStruct((sensors, 2 * modes), BF16),
-            jax.ShapeDtypeStruct((1, sensors), F32),
+            jax.ShapeDtypeStruct((blocks, sensors), BF16),
             jax.ShapeDtypeStruct((8, modes), F32),
         ),
-        in_specs=in_vmem(4),
+        in_specs=[pl.BlockSpec(memory_space=pl.ANY)] + in_vmem(3),
         out_specs=tuple(in_vmem(4)),
-        compiler_params=pltpu.CompilerParams(vmem_limit_bytes=24 * 2**20),
+        scratch_shapes=[pltpu.VMEM((sensors, modes), F32), pltpu.SemaphoreType.DMA((COPIES,))],
+        compiler_params=pltpu.CompilerParams(vmem_limit_bytes=44 * 2**20),
         cost_estimate=pl.CostEstimate(flops=2 * sensors * modes, bytes_accessed=12 * sensors * modes, transcendentals=sensors),
         name="prepare",
-    )(sensor_basis, noise_row, mode_rate.reshape(1, modes), mode_var.reshape(1, modes))
+    )
+    block_row = block_of_sensor.reshape(1, sensors)
+    rate_row = mode_rate.reshape(1, modes)
+    var_row = mode_var.reshape(1, modes)
+
+    pieces, prepared = exchange(
+        observations,
+        block_mask,
+        count,
+        lambda noise: sensor_basis * lax.rsqrt(noise)[:, None],
+        lambda scaled: prepare(scaled, block_row, rate_row, var_row),
+        noise_var,
+    )
+    scaled_t, scaled, onehot, coefs = prepared
 
     square = pltpu.VMEM((modes, modes), F32)
     field, variances, misfit, bound = pl.pallas_call(
-        functools.partial(filter_kernel, count=count, local=local, blocks=blocks),
+        functools.partial(filter_kernel, count=count, local=local, blocks=blocks, parts=len(pieces)),
         out_shape=(
             jax.ShapeDtypeStruct((local, sensors), F32),
             jax.ShapeDtypeStruct((local, 2 * modes), F32),
             jax.ShapeDtypeStruct((1, 1), F32),
             jax.ShapeDtypeStruct((1, 1), F32),
         ),
-        in_specs=[pl.BlockSpec(memory_space=pltpu.SMEM)] + in_vmem(7),
+        in_specs=[pl.BlockSpec(memory_space=pltpu.SMEM)] + in_vmem(len(pieces) + 5),
         out_specs=tuple(in_vmem(4)),
         scratch_shapes=[
             square,
@@ -397,6 +451,7 @@
             pltpu.VMEM((2, modes, modes), F32),
             pltpu.VMEM((4, modes, modes), F32),
             square,
+            pltpu.VMEM((1, sensors), F32),
             pltpu.VMEM((steps, sensors), F32),
             pltpu.VMEM((steps, sensors), F32),
             pltpu.VMEM((steps, modes), F32),
@@ -405,17 +460,17 @@
             pltpu.VMEM((8, modes), F32),
             pltpu.VMEM((steps, LANES), F32),
         ],
-        compiler_params=pltpu.CompilerParams(vmem_limit_bytes=40 * 2**20),
+        compiler_params=pltpu.CompilerParams(vmem_limit_bytes=20 * 2**20),
         cost_estimate=pl.CostEstimate(flops=steps * sensors * modes * 512, bytes_accessed=8 * sensors * modes, transcendentals=0),
         name="filter",
-    )(position.reshape(1), arrived, block_of_sensor.reshape(1, sensors), scaled_t, scaled, root, noise_row, coefs)
+    )(position.reshape(1), *pieces, onehot, scaled_t, scaled, noise_row, coefs)
 
     step_ids = jnp.arange(steps, dtype=jnp.int32)
     order = slot_of((step_ids // local) ^ position, count, local) + step_ids % local
     field, variances, misfit = lax.cond(
         bound[0, 0] <= 1.0,
         lambda: (field, variances, misfit),
-        lambda: careful(order, local, arrived, block_of_sensor, sensor_basis, noise_var, mode_rate, mode_var),
+        lambda: careful(order, local, blocks, jnp.concatenate(pieces, axis=0), block_of_sensor, sensor_basis, noise_var, mode_rate, mode_var),
     )
     return (field, variances, misfit.reshape(1))
 

time: 57.9 us -> 44.2 us (0.76)
  local copies, waits for them, and re-layouts: 11.5 us -> 0.81 us
  other arithmetic: 2.28 us -> 5.64 us
  Pallas kernels: 25.5 us -> 22.5 us
  waiting for transfers between devices: 5.69 us -> 2.72 us
    unnamed x16 -> x8, local copies, waits for them, and re-layouts: 8.29 us -> 0.02 us
    mul x0 -> x1, other arithmetic: none -> 4.16 us  [on_device(): sensor_basis * lax.rsqrt(noise)[:, None]]
    concatenate x2 -> x0, local copies, waits for them, and re-layouts: 3.18 us -> none  [exchange(): rows = jnp.concatenate(pieces, axis=0)]
    ppermute x5 -> x6, waiting for transfers between devices: 5.69 us -> 2.72 us  [swap(): return lax.ppermute(array, AXIS, [(p, p ^ flip) for p in range(count)])]
    pallas_call x1, Pallas kernels: 4.54 us -> 2.78 us  [on_device(): prepare(scaled, block_row, rate_row, var_row)]
    pallas_call x1, Pallas kernels: 21 us -> 19.8 us  [on_device(): pl.pallas_call(functools.partial(filter_kernel, count=count, local=local,...]
    concatenate x2, other arithmetic: 1.61 us -> 0.79 us  [exchange(): rows = pieces[0] if turn == 0 else jnp.concatenate(pieces, axis=0)]
    rsqrt x0 -> x1, local copies, waits for them, and re-layouts: none -> 0.77 us  [on_device(): lax.rsqrt(noise)[:, None]]
  transfers between devices with their start and end apart: 5 -> 6, of which waited for: 4 -> 1; matrix products, arithmetic and copies ran while one was open for 0% -> 13% of each run, Pallas kernels for 8% -> 6%
where the time goes in v2:
time: 44.2 us; the launch traced here: 43.9 us
  Pallas kernels  22.5 us (51%)
  starting transfers between devices  8.88 us (20%)
  other arithmetic  5.64 us (13%)
  waiting for transfers between devices  2.72 us (6%)
  between operations  2.47 us (6%)
  loops' own time  0.88 us (2%)
  local copies, waits for them, and re-layouts  0.81 us (2%)
    pallas_call x1, Pallas kernels, on_device(): pl.pallas_call(functools.partial(filter_kernel, count=count, local=local,...  19.8 us
    ppermute x6, starting transfers between devices, swap(): return lax.ppermute(array, AXIS, [(p, p ^ flip) for p in range(count)])  8.88 us
    mul x1, other arithmetic, on_device(): sensor_basis * lax.rsqrt(noise)[:, None]  4.16 us
    pallas_call x1, Pallas kernels, on_device(): prepare(scaled, block_row, rate_row, var_row)  2.78 us
    ppermute x6, waiting for transfers between devices, swap(): return lax.ppermute(array, AXIS, [(p, p ^ flip) for p in range(count)])  2.72 us
  transfers between devices with their start and end apart: 6, of which 1 were waited for; matrix products, arithmetic and copies ran while one was open for 13% of the time, Pallas kernels for 6%

profile of v2, /device:TPU:1, one launch (start us, length us, event | category | flops | bytes accessed | tf_op | source)
XLA Modules:
  0.0 43.9 jit_solution(1133739531516742998)
XLA Ops:
  0.6 3.2 %collective-permute-start = (f32[1,8192]{1,0:T(1,128)}, f32[1,8192]{1,0:T(1,128)S(1)}, u32[]{:S(2)}, u32[]{:S(2)}) collective-permute-start(f32[1,8192]{1,0:T(1,128)} %param.12), channel_id=1, source_target_pairs={{0,8},{1,9},{2,10},{3,11},{4,12},{5,13},{6,14},{7,15},{8,0},{9,1},... | collective-permute-start | bytes 98312 | tf_op jit(solution)/shard_map/ppermute | solution.py:36
  3.8 0.1 collective-permute-start.1
  3.9 0.7 %convert_element_type.22 = f32[1,64]{1,0:T(1,128)S(1)} convert(s32[1,64]{1,0:T(1,128)} %param.13) | non-fusion elementwise | flops 64 | bytes 512 | tf_op jit(solution)/shard_map/convert_element_type | solution.py:41
  4.6 2.7 %collective-permute-done.1 = s32[1,64]{1,0:T(1,128)S(1)} collective-permute-done((s32[1,64]{1,0:T(1,128)}, s32[1,64]{1,0:T(1,128)S(1)}, u32[]{:S(2)}, u32[]{:S(2)}) %collective-permute-start.1) | collective-permute-done | bytes 288 | tf_op jit(solution)/shard_map/ppermute | solution.py:36
  7.3 0.0 collective-permute-done
  7.3 0.8 %fusion.76 = f32[2,72,128]{2,1,0:T(8,128)S(1)} fusion(f32[1,1,128]{2,1,0:T(1,128)S(1)} %pad_bitcast_fusion, f32[1,1,128]{2,1,0:T(1,128)S(1)} %pad_bitcast_fusion.1, f32[1,64,128]{2,1,0:T(8,128)S(1)} %bitcast.186, f32[1,64,128]{2,1,0:T(8,128)} %bitcast.185), kind=kLoop, calls=%fused_computation.142 | loop fusion | flops 221184 | bytes 140288 | tf_op jit(solution)/shard_map/concatenate | solution.py:52
  8.1 1.2 %collective-permute-start.2 = (f32[2,72,128]{2,1,0:T(8,128)S(1)}, f32[2,72,128]{2,1,0:T(8,128)S(1)}, u32[]{:S(2)}, u32[]{:S(2)}) collective-permute-start(f32[2,72,128]{2,1,0:T(8,128)S(1)} %fusion.76), channel_id=1, source_target_pairs={{0,2},{1,3},{2,0},{3,1},{4,6},{5,7},{6,4},{7,5},{8,10},{9,11},{10,... | collective-permute-start | bytes 221192 | tf_op jit(solution)/shard_map/ppermute | solution.py:36
  9.3 1.2 %collective-permute-start.3 = (f32[2,72,128]{2,1,0:T(8,128)S(1)}, f32[2,72,128]{2,1,0:T(8,128)S(1)}, u32[]{:S(2)}, u32[]{:S(2)}) collective-permute-start(f32[2,72,128]{2,1,0:T(8,128)S(1)} %fusion.76), channel_id=1, source_target_pairs={{0,4},{1,5},{2,6},{3,7},{4,0},{5,1},{6,2},{7,3},{8,12},{9,13},{10,... | collective-permute-start | bytes 221192 | tf_op jit(solution)/shard_map/ppermute | solution.py:36
  10.6 0.2 collective-permute-start.4
  10.7 0.8 %rsqrt.3 = f32[8192]{0:T(1024)S(1)} rsqrt(f32[8192]{0:T(1024)} %param.16) | non-fusion elementwise | bytes 65536 | tf_op jit(solution)/shard_map/rsqrt | solution.py:429
  11.5 0.0 copy-start
  11.5 0.0 copy-start.2
  11.5 0.0 copy-start.3
  11.6 4.2 %broadcast_multiply_fusion.basis_ref = f32[8192,128]{1,0:T(8,128)} fusion(f32[8192,128]{1,0:T(8,128)} %param.15, f32[8192]{0:T(1024)S(1)} %rsqrt.3), kind=kLoop, calls=%fused_computation.139 | loop fusion | flops 1048576 | bytes 8421376 | tf_op jit(solution)/shard_map/mul | solution.py:429
  15.7 0.0 copy-start.1
  15.7 0.0 collective-permute-done.2
  15.7 0.0 collective-permute-done.3
  15.7 0.0 collective-permute-done.4
  15.8 3.0 %collective-permute-start.5 = (f32[8,72,128]{2,1,0:T(8,128)S(1)}, f32[8,72,128]{2,1,0:T(8,128)S(1)}, u32[]{:S(2)}, u32[]{:S(2)}) collective-permute-start(f32[8,72,128]{2,1,0:T(8,128)S(1)} %pad_maximum_fusion.2.refs_0_), channel_id=1, source_target_pairs={{0,1},{1,0},{2,3},{3,2},{4,5},{5,4},{6,7},{7,6},{8,9},{9,8},{10,11... | collective-permute-start | bytes 884744 | tf_op jit(solution)/shard_map/ppermute | solution.py:36
  18.7 0.0 copy-done
  18.7 0.0 copy-done.2
  18.7 0.0 copy-done.3
  18.7 2.8 %prepare.1 = (bf16[256,8192]{1,0:T(8,128)(2,1)S(1)}, bf16[8192,256]{1,0:T(8,128)(2,1)S(1)}, bf16[64,8192]{1,0:T(8,128)(2,1)S(1)}, f32[8,128]{1,0:T(8,128)S(1)}) custom-call(f32[8192,128]{1,0:T(8,128)} %broadcast_multiply_fusion.basis_ref, s32[1,8192]{1,0:T(1,128)S(1)} %bitcast.184, f32[1,128]{1,0:T(1,128)S(1)} %bitcast.189, f32[1,128]{1,0:T(1,128)S(1)} %bitcast.190), custom_call_target="tpu_custom_call" | custom-call | flops 2097152 | bytes 12582912 | tf_op jit(solution)/shard_map/prepare/pallas_call | solution.py:430
  21.5 0.0 collective-permute-done.5.refs_1_
  21.5 0.0 copy-done.1
  21.5 19.8 %filter.1 = (f32[1,8192]{1,0:T(1,128)}, f32[1,256]{1,0:T(1,128)}, f32[1,1]{1,0:T(1,128)}, f32[1,1]{1,0:T(1,128)}) custom-call(s32[1]{0:T(128)} %bitcast.3.position_ref, f32[8,72,128]{2,1,0:T(8,128)S(1)} %pad_maximum_fusion.2.refs_0_, f32[8,72,128]{2,1,0:T(8,128)S(1)} %collective-permute-done.5.refs_1_, bf16[64,8192]{1,0:T(8,128)(2,1)S(1)} %get-tuple-element.195.refs_2_, ...), custom_call_target="tpu_custom_call" | custom-call | flops 8589934592 | bytes 8388608 | tf_op jit(solution)/shard_map/filter/pallas_call | solution.py:436
  41.9 0.9 %conditional.1 = (f32[1,8192]{1,0:T(1,128)}, f32[1,256]{1,0:T(1,128)}, f32[1]{0:T(128)}) conditional(s32[]{:T(128)} %bitcast.12, (f32[8,72,128]{2,1,0:T(8,128)S(1)}, f32[8,72,128]{2,1,0:T(8,128)S(1)}, s32[]{:T(128)}, s32[16]{0:T(128)S(1)}, s32[8192]{0:T(1024)S(1)}, /*index=5*/f32[8192]{0:T(1024)S(1)}, f32[128]{0:T(128)S(1)}, f32[128]{0:T(128)S(1)}, ...), branch_computations={%region_0.9_spmd, %region_8.10_spmd} | conditional | flops 3139522560 | bytes 33127896 | solution.py:470
  (5 shorter events, 0.0 us)
Async XLA Ops:
  0.6 6.7 %collective-permute-start = (f32[1,8192]{1,0:T(1,128)}, f32[1,8192]{1,0:T(1,128)S(1)}, u32[]{:S(2)}, u32[]{:S(2)}) collective-permute-start(f32[1,8192]{1,0:T(1,128)} %param.12), channel_id=1, source_target_pairs={{0,8},{1,9},{2,10},{3,11},{4,12},{5,13},{6,14},{7,15},{8,0},{9,1},... | collective-permute-start | bytes 98312 | tf_op jit(solution)/shard_map/ppermute | solution.py:36
  3.8 3.5 %collective-permute-start.1 = (s32[1,64]{1,0:T(1,128)}, s32[1,64]{1,0:T(1,128)S(1)}, u32[]{:S(2)}, u32[]{:S(2)}) collective-permute-start(s32[1,64]{1,0:T(1,128)} %param.13), channel_id=1, source_target_pairs={{0,8},{1,9},{2,10},{3,11},{4,12},{5,13},{6,14},{7,15},{8,0},{9,1},... | collective-permute-start | bytes 776 | tf_op jit(solution)/shard_map/ppermute | solution.py:36
  8.1 7.6 %collective-permute-start.2 = (f32[2,72,128]{2,1,0:T(8,128)S(1)}, f32[2,72,128]{2,1,0:T(8,128)S(1)}, u32[]{:S(2)}, u32[]{:S(2)}) collective-permute-start(f32[2,72,128]{2,1,0:T(8,128)S(1)} %fusion.76), channel_id=1, source_target_pairs={{0,2},{1,3},{2,0},{3,1},{4,6},{5,7},{6,4},{7,5},{8,10},{9,11},{10,... | collective-permute-start | bytes 221192 | tf_op jit(solution)/shard_map/ppermute | solution.py:36
  9.3 6.4 %collective-permute-start.3 = (f32[2,72,128]{2,1,0:T(8,128)S(1)}, f32[2,72,128]{2,1,0:T(8,128)S(1)}, u32[]{:S(2)}, u32[]{:S(2)}) collective-permute-start(f32[2,72,128]{2,1,0:T(8,128)S(1)} %fusion.76), channel_id=1, source_target_pairs={{0,4},{1,5},{2,6},{3,7},{4,0},{5,1},{6,2},{7,3},{8,12},{9,13},{10,... | collective-permute-start | bytes 221192 | tf_op jit(solution)/shard_map/ppermute | solution.py:36
  10.6 5.1 %collective-permute-start.4 = (f32[2,72,128]{2,1,0:T(8,128)S(1)}, f32[2,72,128]{2,1,0:T(8,128)S(1)}, u32[]{:S(2)}, u32[]{:S(2)}) collective-permute-start(f32[2,72,128]{2,1,0:T(8,128)S(1)} %fusion.76), channel_id=1, source_target_pairs={{0,6},{1,7},{2,4},{3,5},{4,2},{5,3},{6,0},{7,1},{8,14},{9,15},{10,... | collective-permute-start | bytes 221192 | tf_op jit(solution)/shard_map/ppermute | solution.py:36
  11.5 7.2 %copy-start = (s32[8192]{0:T(1024)S(1)}, s32[8192]{0:T(1024)}, u32[]{:S(2)}) copy-start(s32[8192]{0:T(1024)} %param.14) | copy-start | bytes 98308
  11.5 7.2 %copy-start.2 = (f32[128]{0:T(128)S(1)}, f32[128]{0:T(128)}, u32[]{:S(2)}) copy-start(f32[128]{0:T(128)} %param.17) | copy-start | bytes 1540
  11.5 7.2 %copy-start.3 = (f32[128]{0:T(128)S(1)}, f32[128]{0:T(128)}, u32[]{:S(2)}) copy-start(f32[128]{0:T(128)} %param.18) | copy-start | bytes 1540
  15.7 5.8 %copy-start.1 = (f32[8192]{0:T(1024)S(1)}, f32[8192]{0:T(1024)}, u32[]{:S(2)}) copy-start(f32[8192]{0:T(1024)} %param.16) | copy-start | bytes 98308
  15.8 5.7 %collective-permute-start.5 = (f32[8,72,128]{2,1,0:T(8,128)S(1)}, f32[8,72,128]{2,1,0:T(8,128)S(1)}, u32[]{:S(2)}, u32[]{:S(2)}) collective-permute-start(f32[8,72,128]{2,1,0:T(8,128)S(1)} %pad_maximum_fusion.2.refs_0_), channel_id=1, source_target_pairs={{0,1},{1,0},{2,3},{3,2},{4,5},{5,4},{6,7},{7,6},{8,9},{9,8},{10,11... | collective-permute-start | bytes 884744 | tf_op jit(solution)/shard_map/ppermute | solution.py:36

commit v3 on v2

--- a/solution.py
+++ b/solution.py
@@ -15,6 +15,7 @@
 COPIES = 8
 LIMIT_FIRST = 1.0e-2
 LIMIT_LATER = 1.5e-3
+PIVOT_FLOOR = 1.0e-6
 
 
 def gather_rounds(count):
@@ -182,7 +183,6 @@
         field_ref,
         variances_ref,
         misfit_ref,
-        bound_ref,
         p_vv,
         p_vr,
         p_rv,
@@ -198,6 +198,9 @@
         diagonals,
         bounds,
         row_sums,
+        covar,
+        mean_row,
+        rest_g,
     ) = refs[parts:]
     modes = scaled_t_ref.shape[0] // 2
     sensors = scaled_t_ref.shape[1]
@@ -318,6 +321,74 @@
 
     lax.fori_loop(0, steps, one_step, 0)
 
+    def careful_step(step, carry):
+        here = slot(step)
+        total = gram_piece(0, here)
+        for piece in range(1, PIECES):
+            total = total + gram_piece(piece, here)
+        gram_finish(total)
+        low = scaled_t_ref[modes:, :] * mask_rows[pl.ds(here, 1), :].astype(BF16)
+        lam_now[...] = lam_now[...] + dot(low, scaled_ref[:, modes:])
+        floor = PIVOT_FLOOR * jnp.max(diagonal(lam_now[...]), axis=1, keepdims=True)
+        rest_g[...] = grads[pl.ds(here, 1), :]
+
+        def one_pivot(k, inner):
+            lam = lam_now[...]
+            lanes = lax.broadcasted_iota(jnp.int32, (1, modes), 1)
+            pivots = diagonal(lam)
+            pivot = jnp.max(pivots, axis=1, keepdims=True)
+            place = jnp.min(jnp.where(pivots == pivot, lanes, modes), axis=1, keepdims=True)
+            pick = jnp.where(lanes == place, 1.0, 0.0)
+            used = pivot > floor
+            inverse = jnp.where(used, 1.0 / jnp.where(used, pivot, 1.0), 0.0)
+            lam_col = jnp.sum(lam * pick, axis=1, keepdims=True)
+            lam_row = jnp.sum(lam * jnp.sum(eye * pick, axis=1, keepdims=True), axis=0, keepdims=True)
+            seen_row = lam_row * inverse
+            seen_col = lam_col * inverse
+            c_row = jnp.sum(covar[:modes, :] * seen_col, axis=0, keepdims=True)
+            c_col = jnp.sum(covar[:, :modes] * seen_row, axis=1, keepdims=True)
+            spread = jnp.sum(c_row[:, :modes] * seen_row, axis=1, keepdims=True)
+            gain = jnp.where(used, pivot, 0.0) / (1.0 + jnp.where(used, pivot, 0.0) * spread)
+            reading = jnp.sum(rest_g[...] * pick, axis=1, keepdims=True) * inverse
+            surprise = reading - jnp.sum(mean_row[:, :modes] * seen_row, axis=1, keepdims=True)
+            mean_row[...] = mean_row[...] + c_row * (gain * surprise)
+            covar[...] = covar[...] - c_col * (c_row * gain)
+            rest_g[...] = rest_g[...] - lam_row * reading
+            lam_now[...] = lam - lam_col * seen_row
+            return inner
+
+        lax.fori_loop(0, modes, one_pivot, 0)
+        c_vv = covar[:modes, :modes]
+        c_vr = covar[:modes, modes:]
+        c_rv = covar[modes:, :modes]
+        c_rr = covar[modes:, modes:]
+        mean_v = mean_row[:, :modes]
+        mean_r = mean_row[:, modes:]
+        means[pl.ds(here, 1), :] = mean_v
+        diagonals[pl.ds(here, 1), :] = jnp.concatenate([diagonal(c_vv), diagonal(c_rr)], axis=1)
+        mean_row[...] = jnp.concatenate([coef(0) * mean_v + coef(1) * mean_r, coef(2) * mean_v + coef(3) * mean_r], axis=1)
+        a, b, c, d = columns[0], columns[1], columns[2], columns[3]
+        g_vv = a * c_vv + b * c_rv
+        g_vr = a * c_vr + b * c_rr
+        g_rv = c * c_vv + d * c_rv
+        g_rr = c * c_vr + d * c_rr
+        covar[:modes, :modes] = g_vv * coef(0) + g_vr * coef(1) + eye * coef(4)
+        covar[:modes, modes:] = g_vv * coef(2) + g_vr * coef(3) + eye * coef(5)
+        covar[modes:, :modes] = g_rv * coef(0) + g_rr * coef(1) + eye * coef(5)
+        covar[modes:, modes:] = g_rv * coef(2) + g_rr * coef(3) + eye * coef(6)
+        return carry
+
+    limits = jnp.where(lax.broadcasted_iota(jnp.int32, bounds.shape, 0) == 0, LIMIT_FIRST**-2.0, LIMIT_LATER**-2.0)
+    settled = jnp.max(jnp.sum(bounds[...] * limits, axis=1, keepdims=True)) <= 1.0
+
+    @pl.when(jnp.logical_not(settled))
+    def _():
+        covar[...] = jnp.zeros(covar.shape, F32)
+        covar[:modes, :modes] = eye * coef(7)
+        covar[modes:, modes:] = eye * coef(7)
+        mean_row[...] = jnp.zeros(mean_row.shape, F32)
+        lax.fori_loop(0, steps, careful_step, 0)
+
     m_high, m_low = split(means[...])
     m_split = jnp.concatenate(
         [jnp.concatenate([m_high, m_high], axis=1), jnp.concatenate([m_low, m_low], axis=1)], axis=0
@@ -335,59 +406,6 @@
 
     lane_total = lax.fori_loop(0, steps, add_row, jnp.zeros((1, LANES), F32))
     misfit_ref[...] = jnp.sum(lane_total, axis=1, keepdims=True) / (steps * sensors)
-    worst_first = jnp.sum(bounds[0:1], axis=1, keepdims=True) / (LIMIT_FIRST * LIMIT_FIRST)
-    worst_later = jnp.sum(bounds[1:2], axis=1, keepdims=True) / (LIMIT_LATER * LIMIT_LATER)
-    bound_ref[...] = jnp.maximum(worst_first, worst_later)
-
-
-def matmul(left, right):
-    return jnp.dot(left, right, precision=lax.Precision.HIGHEST, preferred_element_type=F32)
-
-
-def careful(order, local, blocks, arrived, block_of_sensor, sensor_basis, noise_var, mode_rate, mode_var):
-    sensors, modes = sensor_basis.shape
-    chunks = sensors // LANES
-    in_time = arrived[order]
-    observations = in_time[:, :chunks, :].reshape(-1, sensors)
-    block_mask = in_time[:, chunks, :blocks]
-    steps = observations.shape[0]
-    f_vv, f_vr, f_rv, f_rr, root_value, root_cross, root_rate, sigma_vec = transition(mode_rate, mode_var)
-    zero = jnp.zeros((modes, modes), F32)
-    trans_mat = jnp.block([[jnp.diag(f_vv), jnp.diag(f_vr)], [jnp.diag(f_rv), jnp.diag(f_rr)]])
-    lower_mat = jnp.block([[jnp.diag(root_value), zero], [jnp.diag(root_cross), jnp.diag(root_rate)]])
-    noise_mat = matmul(lower_mat, lower_mat.T)
-    stationary = jnp.diag(jnp.concatenate([sigma_vec * sigma_vec, sigma_vec * sigma_vec]))
-    onehot = (block_of_sensor[:, None] == jnp.arange(blocks, dtype=jnp.int32)[None, :]).astype(F32)
-    weights = matmul(block_mask, onehot.T) / noise_var[None, :]
-
-    def one_step(carry, inputs):
-        mean_vec, covar = carry
-        weight_row, reading_row, step = inputs
-        info_mat = matmul(sensor_basis.T * weight_row[None, :], sensor_basis)
-        grad_vec = matmul((weight_row * reading_row)[None, :], sensor_basis)[0]
-        trans_eff = jnp.where(step == 0, 0.0, trans_mat)
-        noise_eff = jnp.where(step == 0, stationary, noise_mat)
-        pred_mean = matmul(trans_eff, mean_vec[:, None])[:, 0]
-        pred_cov = matmul(matmul(trans_eff, covar), trans_eff.T) + noise_eff
-        factor_p = jnp.linalg.cholesky(pred_cov)
-        top_rows = factor_p[:modes]
-        inner = jnp.eye(2 * modes, dtype=F32) + matmul(matmul(top_rows.T, info_mat), top_rows)
-        factor_m = jnp.linalg.cholesky(inner)
-        solved = jax.scipy.linalg.solve_triangular(factor_m, factor_p.T, lower=True)
-        new_cov = matmul(solved.T, solved)
-        pull = grad_vec - matmul(info_mat, pred_mean[:modes, None])[:, 0]
-        new_mean = pred_mean + matmul(new_cov[:, :modes], pull[:, None])[:, 0]
-        return ((new_mean, new_cov), (new_mean, jnp.diagonal(new_cov)))
-
-    start = (jnp.zeros((2 * modes,), F32), jnp.zeros((2 * modes, 2 * modes), F32))
-    step_ids = jnp.arange(steps, dtype=jnp.int32)
-    _, (means, variances) = lax.scan(one_step, start, (weights, observations, step_ids))
-    field = matmul(means[:, :modes], sensor_basis.T)
-    misfit = jnp.sum(weights * (observations - field) ** 2) / (steps * sensors)
-    own = lax.axis_index(AXIS) * local
-    own_field = lax.dynamic_slice_in_dim(field, own, local, 0)
-    own_variances = lax.dynamic_slice_in_dim(variances, own, local, 0)
-    return (own_field, own_variances, misfit.reshape(1, 1))
 
 
 def in_vmem(count):
@@ -433,16 +451,15 @@
     scaled_t, scaled, onehot, coefs = prepared
 
     square = pltpu.VMEM((modes, modes), F32)
-    field, variances, misfit, bound = pl.pallas_call(
+    field, variances, misfit = pl.pallas_call(
         functools.partial(filter_kernel, count=count, local=local, blocks=blocks, parts=len(pieces)),
         out_shape=(
             jax.ShapeDtypeStruct((local, sensors), F32),
             jax.ShapeDtypeStruct((local, 2 * modes), F32),
             jax.ShapeDtypeStruct((1, 1), F32),
-            jax.ShapeDtypeStruct((1, 1), F32),
         ),
         in_specs=[pl.BlockSpec(memory_space=pltpu.SMEM)] + in_vmem(len(pieces) + 5),
-        out_specs=tuple(in_vmem(4)),
+        out_specs=tuple(in_vmem(3)),
         scratch_shapes=[
             square,
             square,
@@ -459,19 +476,15 @@
             pltpu.VMEM((steps, 2 * modes), F32),
             pltpu.VMEM((8, modes), F32),
             pltpu.VMEM((steps, LANES), F32),
+            pltpu.VMEM((2 * modes, 2 * modes), F32),
+            pltpu.VMEM((1, 2 * modes), F32),
+            pltpu.VMEM((1, modes), F32),
         ],
         compiler_params=pltpu.CompilerParams(vmem_limit_bytes=20 * 2**20),
         cost_estimate=pl.CostEstimate(flops=steps * sensors * modes * 512, bytes_accessed=8 * sensors * modes, transcendentals=0),
         name="filter",
     )(position.reshape(1), *pieces, onehot, scaled_t, scaled, noise_row, coefs)
 
-    step_ids = jnp.arange(steps, dtype=jnp.int32)
-    order = slot_of((step_ids // local) ^ position, count, local) + step_ids % local
-    field, variances, misfit = lax.cond(
-        bound[0, 0] <= 1.0,
-        lambda: (field, variances, misfit),
-        lambda: careful(order, local, blocks, jnp.concatenate(pieces, axis=0), block_of_sensor, sensor_basis, noise_var, mode_rate, mode_var),
-    )
     return (field, variances, misfit.reshape(1))
 
 

time: 44.2 us -> 41.7 us (0.943)
  between operations: 2.47 us -> 0.71 us
  loops' own time: 0.88 us -> 0 us
    another operation x1 -> x0, loops' own time: 0.88 us -> none  [on_device(): lax.cond(bound[0, 0] <= 1.0, lambda: (field, variances, misfit), lambda:...]
  transfers between devices with their start and end apart: 6 -> 6, of which waited for: 1 -> 1; matrix products, arithmetic and copies ran while one was open for 13% -> 14% of each run, Pallas kernels for 6% -> 7%
where the time goes in v3:
time: 41.7 us; the launch traced here: 41.4 us
  Pallas kernels  22.6 us (54%)
  starting transfers between devices  8.88 us (21%)
  other arithmetic  5.65 us (14%)
  waiting for transfers between devices  2.72 us (7%)
  local copies, waits for them, and re-layouts  0.8 us (2%)
  between operations  0.71 us (2%)
    pallas_call x1, Pallas kernels, on_device(): pl.pallas_call(functools.partial(filter_kernel, count=count, local=local,...  19.8 us
    ppermute x6, starting transfers between devices, swap(): return lax.ppermute(array, AXIS, [(p, p ^ flip) for p in range(count)])  8.88 us
    mul x1, other arithmetic, on_device(): sensor_basis * lax.rsqrt(noise)[:, None]  4.17 us
    pallas_call x1, Pallas kernels, on_device(): prepare(scaled, block_row, rate_row, var_row)  2.78 us
    ppermute x6, waiting for transfers between devices, swap(): return lax.ppermute(array, AXIS, [(p, p ^ flip) for p in range(count)])  2.72 us
  transfers between devices with their start and end apart: 6, of which 1 were waited for; matrix products, arithmetic and copies ran while one was open for 14% of the time, Pallas kernels for 7%

profile of v3, /device:TPU:1, one launch (start us, length us, event | category | flops | bytes accessed | tf_op | source)
XLA Modules:
  0.0 41.4 jit_solution(10576274368981895005)
XLA Ops:
  0.6 3.2 %collective-permute-start = (f32[1,8192]{1,0:T(1,128)}, f32[1,8192]{1,0:T(1,128)S(1)}, u32[]{:S(2)}, u32[]{:S(2)}) collective-permute-start(f32[1,8192]{1,0:T(1,128)} %param.7), channel_id=1, source_target_pairs={{0,8},{1,9},{2,10},{3,11},{4,12},{5,13},{6,14},{7,15},{8,0},{9,1},... | collective-permute-start | bytes 98312 | tf_op jit(solution)/shard_map/ppermute | solution.py:37
  3.8 0.1 collective-permute-start.1
  3.9 0.7 %convert_element_type.12 = f32[1,64]{1,0:T(1,128)S(1)} convert(s32[1,64]{1,0:T(1,128)} %param.8) | non-fusion elementwise | flops 64 | bytes 512 | tf_op jit(solution)/shard_map/convert_element_type | solution.py:42
  4.6 2.7 %collective-permute-done.1 = s32[1,64]{1,0:T(1,128)S(1)} collective-permute-done((s32[1,64]{1,0:T(1,128)}, s32[1,64]{1,0:T(1,128)S(1)}, u32[]{:S(2)}, u32[]{:S(2)}) %collective-permute-start.1) | collective-permute-done | bytes 288 | tf_op jit(solution)/shard_map/ppermute | solution.py:37
  7.3 0.0 collective-permute-done
  7.3 0.8 %fusion = f32[2,72,128]{2,1,0:T(8,128)S(1)} fusion(f32[1,1,128]{2,1,0:T(1,128)S(1)} %pad_bitcast_fusion, f32[1,1,128]{2,1,0:T(1,128)S(1)} %pad_bitcast_fusion.1, f32[1,64,128]{2,1,0:T(8,128)S(1)} %bitcast.17, f32[1,64,128]{2,1,0:T(8,128)} %bitcast.16), kind=kLoop, calls=%fused_computation.3 | loop fusion | flops 221184 | bytes 140288 | tf_op jit(solution)/shard_map/concatenate | solution.py:53
  8.1 1.2 %collective-permute-start.2 = (f32[2,72,128]{2,1,0:T(8,128)S(1)}, f32[2,72,128]{2,1,0:T(8,128)S(1)}, u32[]{:S(2)}, u32[]{:S(2)}) collective-permute-start(f32[2,72,128]{2,1,0:T(8,128)S(1)} %fusion), channel_id=1, source_target_pairs={{0,2},{1,3},{2,0},{3,1},{4,6},{5,7},{6,4},{7,5},{8,10},{9,11},{10,... | collective-permute-start | bytes 221192 | tf_op jit(solution)/shard_map/ppermute | solution.py:37
  9.3 1.2 %collective-permute-start.3 = (f32[2,72,128]{2,1,0:T(8,128)S(1)}, f32[2,72,128]{2,1,0:T(8,128)S(1)}, u32[]{:S(2)}, u32[]{:S(2)}) collective-permute-start(f32[2,72,128]{2,1,0:T(8,128)S(1)} %fusion), channel_id=1, source_target_pairs={{0,4},{1,5},{2,6},{3,7},{4,0},{5,1},{6,2},{7,3},{8,12},{9,13},{10,... | collective-permute-start | bytes 221192 | tf_op jit(solution)/shard_map/ppermute | solution.py:37
  10.6 0.2 collective-permute-start.4
  10.7 0.8 %rsqrt.3 = f32[8192]{0:T(1024)S(1)} rsqrt(f32[8192]{0:T(1024)} %param.11) | non-fusion elementwise | bytes 65536 | tf_op jit(solution)/shard_map/rsqrt | solution.py:447
  11.5 0.0 copy-start
  11.5 0.0 copy-start.2
  11.5 0.0 copy-start.3
  11.6 4.2 %broadcast_multiply_fusion.basis_ref = f32[8192,128]{1,0:T(8,128)} fusion(f32[8192,128]{1,0:T(8,128)} %param.10, f32[8192]{0:T(1024)S(1)} %rsqrt.3), kind=kLoop, calls=%fused_computation | loop fusion | flops 1048576 | bytes 8421376 | tf_op jit(solution)/shard_map/mul | solution.py:447
  15.7 0.0 copy-start.1
  15.7 0.0 collective-permute-done.2
  15.7 0.0 collective-permute-done.3
  15.7 0.0 collective-permute-done.4
  15.8 3.0 %collective-permute-start.5 = (f32[8,72,128]{2,1,0:T(8,128)S(1)}, f32[8,72,128]{2,1,0:T(8,128)S(1)}, u32[]{:S(2)}, u32[]{:S(2)}) collective-permute-start(f32[8,72,128]{2,1,0:T(8,128)S(1)} %pad_maximum_fusion.refs_0_), channel_id=1, source_target_pairs={{0,1},{1,0},{2,3},{3,2},{4,5},{5,4},{6,7},{7,6},{8,9},{9,8},{10,11... | collective-permute-start | bytes 884744 | tf_op jit(solution)/shard_map/ppermute | solution.py:37
  18.7 0.0 copy-done
  18.7 0.0 copy-done.2
  18.7 0.0 copy-done.3
  18.7 2.8 %prepare.1 = (bf16[256,8192]{1,0:T(8,128)(2,1)S(1)}, bf16[8192,256]{1,0:T(8,128)(2,1)S(1)}, bf16[64,8192]{1,0:T(8,128)(2,1)S(1)}, f32[8,128]{1,0:T(8,128)S(1)}) custom-call(f32[8192,128]{1,0:T(8,128)} %broadcast_multiply_fusion.basis_ref, s32[1,8192]{1,0:T(1,128)S(1)} %bitcast.12, f32[1,128]{1,0:T(1,128)S(1)} %bitcast.14, f32[1,128]{1,0:T(1,128)S(1)} %bitcast.15), custom_call_target="tpu_custom_call" | custom-call | flops 2097152 | bytes 12582912 | tf_op jit(solution)/shard_map/prepare/pallas_call | solution.py:448
  21.5 0.0 collective-permute-done.5.refs_1_
  21.5 0.0 copy-done.1
  21.5 19.8 %filter.1 = (f32[1,8192]{1,0:T(1,128)}, f32[1,256]{1,0:T(1,128)}, f32[1,1]{1,0:T(1,128)}) custom-call(s32[1]{0:T(128)} %bitcast.position_ref, f32[8,72,128]{2,1,0:T(8,128)S(1)} %pad_maximum_fusion.refs_0_, f32[8,72,128]{2,1,0:T(8,128)S(1)} %collective-permute-done.5.refs_1_, bf16[64,8192]{1,0:T(8,128)(2,1)S(1)} %get-tuple-element.18.refs_2_, ...), custom_call_target="tpu_custom_call" | custom-call | flops 8589934592 | bytes 8388608 | tf_op jit(solution)/shard_map/filter/pallas_call | solution.py:454
  (4 shorter events, 0.0 us)
Async XLA Ops:
  0.6 6.7 %collective-permute-start = (f32[1,8192]{1,0:T(1,128)}, f32[1,8192]{1,0:T(1,128)S(1)}, u32[]{:S(2)}, u32[]{:S(2)}) collective-permute-start(f32[1,8192]{1,0:T(1,128)} %param.7), channel_id=1, source_target_pairs={{0,8},{1,9},{2,10},{3,11},{4,12},{5,13},{6,14},{7,15},{8,0},{9,1},... | collective-permute-start | bytes 98312 | tf_op jit(solution)/shard_map/ppermute | solution.py:37
  3.8 3.5 %collective-permute-start.1 = (s32[1,64]{1,0:T(1,128)}, s32[1,64]{1,0:T(1,128)S(1)}, u32[]{:S(2)}, u32[]{:S(2)}) collective-permute-start(s32[1,64]{1,0:T(1,128)} %param.8), channel_id=1, source_target_pairs={{0,8},{1,9},{2,10},{3,11},{4,12},{5,13},{6,14},{7,15},{8,0},{9,1},... | collective-permute-start | bytes 776 | tf_op jit(solution)/shard_map/ppermute | solution.py:37
  8.1 7.6 %collective-permute-start.2 = (f32[2,72,128]{2,1,0:T(8,128)S(1)}, f32[2,72,128]{2,1,0:T(8,128)S(1)}, u32[]{:S(2)}, u32[]{:S(2)}) collective-permute-start(f32[2,72,128]{2,1,0:T(8,128)S(1)} %fusion), channel_id=1, source_target_pairs={{0,2},{1,3},{2,0},{3,1},{4,6},{5,7},{6,4},{7,5},{8,10},{9,11},{10,... | collective-permute-start | bytes 221192 | tf_op jit(solution)/shard_map/ppermute | solution.py:37
  9.3 6.4 %collective-permute-start.3 = (f32[2,72,128]{2,1,0:T(8,128)S(1)}, f32[2,72,128]{2,1,0:T(8,128)S(1)}, u32[]{:S(2)}, u32[]{:S(2)}) collective-permute-start(f32[2,72,128]{2,1,0:T(8,128)S(1)} %fusion), channel_id=1, source_target_pairs={{0,4},{1,5},{2,6},{3,7},{4,0},{5,1},{6,2},{7,3},{8,12},{9,13},{10,... | collective-permute-start | bytes 221192 | tf_op jit(solution)/shard_map/ppermute | solution.py:37
  10.6 5.2 %collective-permute-start.4 = (f32[2,72,128]{2,1,0:T(8,128)S(1)}, f32[2,72,128]{2,1,0:T(8,128)S(1)}, u32[]{:S(2)}, u32[]{:S(2)}) collective-permute-start(f32[2,72,128]{2,1,0:T(8,128)S(1)} %fusion), channel_id=1, source_target_pairs={{0,6},{1,7},{2,4},{3,5},{4,2},{5,3},{6,0},{7,1},{8,14},{9,15},{10,... | collective-permute-start | bytes 221192 | tf_op jit(solution)/shard_map/ppermute | solution.py:37
  11.5 7.2 %copy-start = (s32[8192]{0:T(1024)S(1)}, s32[8192]{0:T(1024)}, u32[]{:S(2)}) copy-start(s32[8192]{0:T(1024)} %param.9) | copy-start | bytes 98308
  11.5 7.2 %copy-start.2 = (f32[128]{0:T(128)S(1)}, f32[128]{0:T(128)}, u32[]{:S(2)}) copy-start(f32[128]{0:T(128)} %param.12) | copy-start | bytes 1540
  11.5 7.2 %copy-start.3 = (f32[128]{0:T(128)S(1)}, f32[128]{0:T(128)}, u32[]{:S(2)}) copy-start(f32[128]{0:T(128)} %param.13) | copy-start | bytes 1540
  15.7 5.8 %copy-start.1 = (f32[8192]{0:T(1024)S(1)}, f32[8192]{0:T(1024)}, u32[]{:S(2)}) copy-start(f32[8192]{0:T(1024)} %param.11) | copy-start | bytes 98308
  15.8 5.7 %collective-permute-start.5 = (f32[8,72,128]{2,1,0:T(8,128)S(1)}, f32[8,72,128]{2,1,0:T(8,128)S(1)}, u32[]{:S(2)}, u32[]{:S(2)}) collective-permute-start(f32[8,72,128]{2,1,0:T(8,128)S(1)} %pad_maximum_fusion.refs_0_), channel_id=1, source_target_pairs={{0,1},{1,0},{2,3},{3,2},{4,5},{5,4},{6,7},{7,6},{8,9},{9,8},{10,11... | collective-permute-start | bytes 884744 | tf_op jit(solution)/shard_map/ppermute | solution.py:37

commit v4 on v3

--- a/solution.py
+++ b/solution.py
@@ -256,9 +256,9 @@
     g_half = first[modes:, :modes] + first[modes:, modes:]
     grads[...] = g_half[:steps] + g_half[steps:]
 
-    def one_step(step, carry):
+    def one_step(step, carry, last=False):
         here = slot(step)
-        ahead = slot(jnp.minimum(step + 1, steps - 1))
+        ahead = slot(step + 1)
         lam = lam_now[...]
         pred_vv = p_vv[...]
         pred_rv = p_rv[...]
@@ -266,12 +266,13 @@
         lam_wide = wide(lam)
         lam_p = dot_three(lam_wide, pred_vv)
         cross = dot_three(lam_wide, p_vr[...])
-        total = gram_piece(0, ahead) + gram_piece(1, ahead)
+        total = None if last else gram_piece(0, ahead) + gram_piece(1, ahead)
         scale = 1.0 / (1.0 + diagonal(lam) * diagonal(pred_vv))
         rest = eye * (1.0 - scale) - lam_p * scale
         scaled_p = jnp.concatenate([pred_vv * scale, pred_rv * scale], axis=0)
         second = dot_split(wide(jnp.concatenate([rest, scaled_p], axis=0)), twice(wide(rest)))
-        total = total + (gram_piece(2, ahead) + gram_piece(3, ahead))
+        if not last:
+            total = total + (gram_piece(2, ahead) + gram_piece(3, ahead))
         rest2 = second[:modes]
         cols1 = scaled_p + second[modes:]
         rest2_high = rest2.astype(BF16)
@@ -279,7 +280,8 @@
         rest4 = dot(rest2_high, rest2_high).astype(BF16)
         rest2_cross = dot(rest2_high, cross_high)
         cols_add = dot(cols1.astype(BF16), rest2_high)
-        total = total + (gram_piece(4, ahead) + gram_piece(5, ahead))
+        if not last:
+            total = total + (gram_piece(4, ahead) + gram_piece(5, ahead))
         cols2 = cols1 + cols_add
         cols2_high, cols2_low = split(cols2)
         cols3 = cols2 + dot(cols2_high, rest4)
@@ -287,7 +289,8 @@
         taken = dot_split(
             jnp.concatenate([cols2_high[modes:], cols2_low[modes:]], axis=1), twice(cross_wide)
         ) + dot(cols_add[modes:].astype(BF16), rest2_cross.astype(BF16))
-        total = total + (gram_piece(6, ahead) + gram_piece(7, ahead))
+        if not last:
+            total = total + (gram_piece(6, ahead) + gram_piece(7, ahead))
         c_rr = pred_rr - taken
         c_vv = cols3[:modes]
         c_rv = cols3[modes:]
@@ -305,6 +308,8 @@
             bounds[pl.ds(jnp.minimum(step, 1), 1), :], jnp.sum(rest4_f32 * rest4_f32, axis=0, keepdims=True)
         )
 
+        if last:
+            return carry
         a, b, c, d = columns[0], columns[1], columns[2], columns[3]
         pred_mean[0] = a * mean_v + b * mean_r
         pred_mean[1] = c * mean_v + d * mean_r
@@ -319,7 +324,8 @@
         gram_finish(total)
         return carry
 
-    lax.fori_loop(0, steps, one_step, 0)
+    lax.fori_loop(0, steps - 1, one_step, 0)
+    one_step(steps - 1, 0, last=True)
 
     def careful_step(step, carry):
         here = slot(step)
@@ -399,12 +405,13 @@
     variances_ref[...] = diagonals[:local, :]
     gap = readings[...] - mask_rows[...] * scaled_field
     squares = gap * gap
-    row_sums[...] = jnp.sum(squares.reshape(steps, sensors // LANES, LANES), axis=1)
-
-    def add_row(step, total):
-        return total + row_sums[pl.ds(slot(step), 1), :]
-
-    lane_total = lax.fori_loop(0, steps, add_row, jnp.zeros((1, LANES), F32))
+    lanes_first = squares[:, :LANES]
+    for chunk in range(1, chunks):
+        lanes_first = lanes_first + squares[:, chunk * LANES : (chunk + 1) * LANES]
+    row_sums[...] = lanes_first
+    lane_total = row_sums[pl.ds(slot(0), 1), :]
+    for step in range(1, steps):
+        lane_total = lane_total + row_sums[pl.ds(slot(step), 1), :]
     misfit_ref[...] = jnp.sum(lane_total, axis=1, keepdims=True) / (steps * sensors)
 
 

time: 41.7 us -> 41.1 us (0.986)
  Pallas kernels: 22.6 us -> 22 us
    pallas_call x1, Pallas kernels: 19.8 us -> 19.3 us  [on_device(): pl.pallas_call(functools.partial(filter_kernel, count=count, local=local,...]
where the time goes in v4:
time: 41.1 us; the launch traced here: 40.8 us
  Pallas kernels  22 us (54%)
  starting transfers between devices  8.88 us (22%)
  other arithmetic  5.65 us (14%)
  waiting for transfers between devices  2.72 us (7%)
  local copies, waits for them, and re-layouts  0.8 us (2%)
  between operations  0.71 us (2%)
    pallas_call x1, Pallas kernels, on_device(): pl.pallas_call(functools.partial(filter_kernel, count=count, local=local,...  19.3 us
    ppermute x6, starting transfers between devices, swap(): return lax.ppermute(array, AXIS, [(p, p ^ flip) for p in range(count)])  8.88 us
    mul x1, other arithmetic, on_device(): sensor_basis * lax.rsqrt(noise)[:, None]  4.17 us
    pallas_call x1, Pallas kernels, on_device(): prepare(scaled, block_row, rate_row, var_row)  2.78 us
    ppermute x6, waiting for transfers between devices, swap(): return lax.ppermute(array, AXIS, [(p, p ^ flip) for p in range(count)])  2.72 us
  transfers between devices with their start and end apart: 6, of which 1 were waited for; matrix products, arithmetic and copies ran while one was open for 14% of the time, Pallas kernels for 7%

profile of v4, /device:TPU:1, one launch (start us, length us, event | category | flops | bytes accessed | tf_op | source)
XLA Modules:
  0.0 40.8 jit_solution(2577255622182262965)
XLA Ops:
  0.6 3.2 %collective-permute-start = (f32[1,8192]{1,0:T(1,128)}, f32[1,8192]{1,0:T(1,128)S(1)}, u32[]{:S(2)}, u32[]{:S(2)}) collective-permute-start(f32[1,8192]{1,0:T(1,128)} %param.7), channel_id=1, source_target_pairs={{0,8},{1,9},{2,10},{3,11},{4,12},{5,13},{6,14},{7,15},{8,0},{9,1},... | collective-permute-start | bytes 98312 | tf_op jit(solution)/shard_map/ppermute | solution.py:37
  3.8 0.1 collective-permute-start.1
  3.9 0.7 %convert_element_type.12 = f32[1,64]{1,0:T(1,128)S(1)} convert(s32[1,64]{1,0:T(1,128)} %param.8) | non-fusion elementwise | flops 64 | bytes 512 | tf_op jit(solution)/shard_map/convert_element_type | solution.py:42
  4.6 2.7 %collective-permute-done.1 = s32[1,64]{1,0:T(1,128)S(1)} collective-permute-done((s32[1,64]{1,0:T(1,128)}, s32[1,64]{1,0:T(1,128)S(1)}, u32[]{:S(2)}, u32[]{:S(2)}) %collective-permute-start.1) | collective-permute-done | bytes 288 | tf_op jit(solution)/shard_map/ppermute | solution.py:37
  7.3 0.0 collective-permute-done
  7.3 0.8 %fusion = f32[2,72,128]{2,1,0:T(8,128)S(1)} fusion(f32[1,1,128]{2,1,0:T(1,128)S(1)} %pad_bitcast_fusion, f32[1,1,128]{2,1,0:T(1,128)S(1)} %pad_bitcast_fusion.1, f32[1,64,128]{2,1,0:T(8,128)S(1)} %bitcast.17, f32[1,64,128]{2,1,0:T(8,128)} %bitcast.16), kind=kLoop, calls=%fused_computation.3 | loop fusion | flops 221184 | bytes 140288 | tf_op jit(solution)/shard_map/concatenate | solution.py:53
  8.1 1.2 %collective-permute-start.2 = (f32[2,72,128]{2,1,0:T(8,128)S(1)}, f32[2,72,128]{2,1,0:T(8,128)S(1)}, u32[]{:S(2)}, u32[]{:S(2)}) collective-permute-start(f32[2,72,128]{2,1,0:T(8,128)S(1)} %fusion), channel_id=1, source_target_pairs={{0,2},{1,3},{2,0},{3,1},{4,6},{5,7},{6,4},{7,5},{8,10},{9,11},{10,... | collective-permute-start | bytes 221192 | tf_op jit(solution)/shard_map/ppermute | solution.py:37
  9.3 1.2 %collective-permute-start.3 = (f32[2,72,128]{2,1,0:T(8,128)S(1)}, f32[2,72,128]{2,1,0:T(8,128)S(1)}, u32[]{:S(2)}, u32[]{:S(2)}) collective-permute-start(f32[2,72,128]{2,1,0:T(8,128)S(1)} %fusion), channel_id=1, source_target_pairs={{0,4},{1,5},{2,6},{3,7},{4,0},{5,1},{6,2},{7,3},{8,12},{9,13},{10,... | collective-permute-start | bytes 221192 | tf_op jit(solution)/shard_map/ppermute | solution.py:37
  10.6 0.2 collective-permute-start.4
  10.7 0.8 %rsqrt.3 = f32[8192]{0:T(1024)S(1)} rsqrt(f32[8192]{0:T(1024)} %param.11) | non-fusion elementwise | bytes 65536 | tf_op jit(solution)/shard_map/rsqrt | solution.py:454
  11.5 0.0 copy-start
  11.5 0.0 copy-start.2
  11.5 0.0 copy-start.3
  11.6 4.2 %broadcast_multiply_fusion.basis_ref = f32[8192,128]{1,0:T(8,128)} fusion(f32[8192,128]{1,0:T(8,128)} %param.10, f32[8192]{0:T(1024)S(1)} %rsqrt.3), kind=kLoop, calls=%fused_computation | loop fusion | flops 1048576 | bytes 8421376 | tf_op jit(solution)/shard_map/mul | solution.py:454
  15.7 0.0 copy-start.1
  15.7 0.0 collective-permute-done.2
  15.7 0.0 collective-permute-done.3
  15.7 0.0 collective-permute-done.4
  15.8 3.0 %collective-permute-start.5 = (f32[8,72,128]{2,1,0:T(8,128)S(1)}, f32[8,72,128]{2,1,0:T(8,128)S(1)}, u32[]{:S(2)}, u32[]{:S(2)}) collective-permute-start(f32[8,72,128]{2,1,0:T(8,128)S(1)} %pad_maximum_fusion.refs_0_), channel_id=1, source_target_pairs={{0,1},{1,0},{2,3},{3,2},{4,5},{5,4},{6,7},{7,6},{8,9},{9,8},{10,11... | collective-permute-start | bytes 884744 | tf_op jit(solution)/shard_map/ppermute | solution.py:37
  18.7 0.0 copy-done
  18.7 0.0 copy-done.2
  18.7 0.0 copy-done.3
  18.7 2.8 %prepare.1 = (bf16[256,8192]{1,0:T(8,128)(2,1)S(1)}, bf16[8192,256]{1,0:T(8,128)(2,1)S(1)}, bf16[64,8192]{1,0:T(8,128)(2,1)S(1)}, f32[8,128]{1,0:T(8,128)S(1)}) custom-call(f32[8192,128]{1,0:T(8,128)} %broadcast_multiply_fusion.basis_ref, s32[1,8192]{1,0:T(1,128)S(1)} %bitcast.12, f32[1,128]{1,0:T(1,128)S(1)} %bitcast.14, f32[1,128]{1,0:T(1,128)S(1)} %bitcast.15), custom_call_target="tpu_custom_call" | custom-call | flops 2097152 | bytes 12582912 | tf_op jit(solution)/shard_map/prepare/pallas_call | solution.py:455
  21.5 0.0 collective-permute-done.5.refs_1_
  21.5 0.0 copy-done.1
  21.5 19.3 %filter.1 = (f32[1,8192]{1,0:T(1,128)}, f32[1,256]{1,0:T(1,128)}, f32[1,1]{1,0:T(1,128)}) custom-call(s32[1]{0:T(128)} %bitcast.position_ref, f32[8,72,128]{2,1,0:T(8,128)S(1)} %pad_maximum_fusion.refs_0_, f32[8,72,128]{2,1,0:T(8,128)S(1)} %collective-permute-done.5.refs_1_, bf16[64,8192]{1,0:T(8,128)(2,1)S(1)} %get-tuple-element.18.refs_2_, ...), custom_call_target="tpu_custom_call" | custom-call | flops 8589934592 | bytes 8388608 | tf_op jit(solution)/shard_map/filter/pallas_call | solution.py:461
  (4 shorter events, 0.0 us)
Async XLA Ops:
  0.6 6.7 %collective-permute-start = (f32[1,8192]{1,0:T(1,128)}, f32[1,8192]{1,0:T(1,128)S(1)}, u32[]{:S(2)}, u32[]{:S(2)}) collective-permute-start(f32[1,8192]{1,0:T(1,128)} %param.7), channel_id=1, source_target_pairs={{0,8},{1,9},{2,10},{3,11},{4,12},{5,13},{6,14},{7,15},{8,0},{9,1},... | collective-permute-start | bytes 98312 | tf_op jit(solution)/shard_map/ppermute | solution.py:37
  3.8 3.5 %collective-permute-start.1 = (s32[1,64]{1,0:T(1,128)}, s32[1,64]{1,0:T(1,128)S(1)}, u32[]{:S(2)}, u32[]{:S(2)}) collective-permute-start(s32[1,64]{1,0:T(1,128)} %param.8), channel_id=1, source_target_pairs={{0,8},{1,9},{2,10},{3,11},{4,12},{5,13},{6,14},{7,15},{8,0},{9,1},... | collective-permute-start | bytes 776 | tf_op jit(solution)/shard_map/ppermute | solution.py:37
  8.1 7.6 %collective-permute-start.2 = (f32[2,72,128]{2,1,0:T(8,128)S(1)}, f32[2,72,128]{2,1,0:T(8,128)S(1)}, u32[]{:S(2)}, u32[]{:S(2)}) collective-permute-start(f32[2,72,128]{2,1,0:T(8,128)S(1)} %fusion), channel_id=1, source_target_pairs={{0,2},{1,3},{2,0},{3,1},{4,6},{5,7},{6,4},{7,5},{8,10},{9,11},{10,... | collective-permute-start | bytes 221192 | tf_op jit(solution)/shard_map/ppermute | solution.py:37
  9.3 6.4 %collective-permute-start.3 = (f32[2,72,128]{2,1,0:T(8,128)S(1)}, f32[2,72,128]{2,1,0:T(8,128)S(1)}, u32[]{:S(2)}, u32[]{:S(2)}) collective-permute-start(f32[2,72,128]{2,1,0:T(8,128)S(1)} %fusion), channel_id=1, source_target_pairs={{0,4},{1,5},{2,6},{3,7},{4,0},{5,1},{6,2},{7,3},{8,12},{9,13},{10,... | collective-permute-start | bytes 221192 | tf_op jit(solution)/shard_map/ppermute | solution.py:37
  10.6 5.2 %collective-permute-start.4 = (f32[2,72,128]{2,1,0:T(8,128)S(1)}, f32[2,72,128]{2,1,0:T(8,128)S(1)}, u32[]{:S(2)}, u32[]{:S(2)}) collective-permute-start(f32[2,72,128]{2,1,0:T(8,128)S(1)} %fusion), channel_id=1, source_target_pairs={{0,6},{1,7},{2,4},{3,5},{4,2},{5,3},{6,0},{7,1},{8,14},{9,15},{10,... | collective-permute-start | bytes 221192 | tf_op jit(solution)/shard_map/ppermute | solution.py:37
  11.5 7.2 %copy-start = (s32[8192]{0:T(1024)S(1)}, s32[8192]{0:T(1024)}, u32[]{:S(2)}) copy-start(s32[8192]{0:T(1024)} %param.9) | copy-start | bytes 98308
  11.5 7.2 %copy-start.2 = (f32[128]{0:T(128)S(1)}, f32[128]{0:T(128)}, u32[]{:S(2)}) copy-start(f32[128]{0:T(128)} %param.12) | copy-start | bytes 1540
  11.5 7.2 %copy-start.3 = (f32[128]{0:T(128)S(1)}, f32[128]{0:T(128)}, u32[]{:S(2)}) copy-start(f32[128]{0:T(128)} %param.13) | copy-start | bytes 1540
  15.7 5.8 %copy-start.1 = (f32[8192]{0:T(1024)S(1)}, f32[8192]{0:T(1024)}, u32[]{:S(2)}) copy-start(f32[8192]{0:T(1024)} %param.11) | copy-start | bytes 98308
  15.8 5.7 %collective-permute-start.5 = (f32[8,72,128]{2,1,0:T(8,128)S(1)}, f32[8,72,128]{2,1,0:T(8,128)S(1)}, u32[]{:S(2)}, u32[]{:S(2)}) collective-permute-start(f32[8,72,128]{2,1,0:T(8,128)S(1)} %pad_maximum_fusion.refs_0_), channel_id=1, source_target_pairs={{0,1},{1,0},{2,3},{3,2},{4,5},{5,4},{6,7},{7,6},{8,9},{9,8},{10,11... | collective-permute-start | bytes 884744 | tf_op jit(solution)/shard_map/ppermute | solution.py:37

commit v5 on v4

--- a/solution.py
+++ b/solution.py
@@ -12,7 +12,7 @@
 AXIS = "tm"
 LANES = 128
 PIECES = 8
-COPIES = 8
+COPIES = 4
 LIMIT_FIRST = 1.0e-2
 LIMIT_LATER = 1.5e-3
 PIVOT_FLOOR = 1.0e-6

time: 41.1 us -> 41 us (level)
  no operation moved by 1% of the time
where the time goes in v5:
time: 41 us; the launch traced here: 40.7 us
  Pallas kernels  21.9 us (53%)
  starting transfers between devices  8.88 us (22%)
  other arithmetic  5.65 us (14%)
  waiting for transfers between devices  2.72 us (7%)
  local copies, waits for them, and re-layouts  0.8 us (2%)
  between operations  0.71 us (2%)
    pallas_call x1, Pallas kernels, on_device(): pl.pallas_call(functools.partial(filter_kernel, count=count, local=local,...  19.3 us
    ppermute x6, starting transfers between devices, swap(): return lax.ppermute(array, AXIS, [(p, p ^ flip) for p in range(count)])  8.88 us
    mul x1, other arithmetic, on_device(): sensor_basis * lax.rsqrt(noise)[:, None]  4.17 us
    ppermute x6, waiting for transfers between devices, swap(): return lax.ppermute(array, AXIS, [(p, p ^ flip) for p in range(count)])  2.72 us
    pallas_call x1, Pallas kernels, on_device(): prepare(scaled, block_row, rate_row, var_row)  2.67 us
  transfers between devices with their start and end apart: 6, of which 1 were waited for; matrix products, arithmetic and copies ran while one was open for 14% of the time, Pallas kernels for 7%

profile of v5, /device:TPU:1, one launch (start us, length us, event | category | flops | bytes accessed | tf_op | source)
XLA Modules:
  0.0 40.7 jit_solution(13346384889812242847)
XLA Ops:
  0.6 3.2 %collective-permute-start = (f32[1,8192]{1,0:T(1,128)}, f32[1,8192]{1,0:T(1,128)S(1)}, u32[]{:S(2)}, u32[]{:S(2)}) collective-permute-start(f32[1,8192]{1,0:T(1,128)} %param.7), channel_id=1, source_target_pairs={{0,8},{1,9},{2,10},{3,11},{4,12},{5,13},{6,14},{7,15},{8,0},{9,1},... | collective-permute-start | bytes 98312 | tf_op jit(solution)/shard_map/ppermute | solution.py:37
  3.8 0.1 collective-permute-start.1
  3.9 0.7 %convert_element_type.12 = f32[1,64]{1,0:T(1,128)S(1)} convert(s32[1,64]{1,0:T(1,128)} %param.8) | non-fusion elementwise | flops 64 | bytes 512 | tf_op jit(solution)/shard_map/convert_element_type | solution.py:42
  4.6 2.7 %collective-permute-done.1 = s32[1,64]{1,0:T(1,128)S(1)} collective-permute-done((s32[1,64]{1,0:T(1,128)}, s32[1,64]{1,0:T(1,128)S(1)}, u32[]{:S(2)}, u32[]{:S(2)}) %collective-permute-start.1) | collective-permute-done | bytes 288 | tf_op jit(solution)/shard_map/ppermute | solution.py:37
  7.3 0.0 collective-permute-done
  7.3 0.8 %fusion = f32[2,72,128]{2,1,0:T(8,128)S(1)} fusion(f32[1,1,128]{2,1,0:T(1,128)S(1)} %pad_bitcast_fusion, f32[1,1,128]{2,1,0:T(1,128)S(1)} %pad_bitcast_fusion.1, f32[1,64,128]{2,1,0:T(8,128)S(1)} %bitcast.17, f32[1,64,128]{2,1,0:T(8,128)} %bitcast.16), kind=kLoop, calls=%fused_computation.3 | loop fusion | flops 221184 | bytes 140288 | tf_op jit(solution)/shard_map/concatenate | solution.py:53
  8.1 1.2 %collective-permute-start.2 = (f32[2,72,128]{2,1,0:T(8,128)S(1)}, f32[2,72,128]{2,1,0:T(8,128)S(1)}, u32[]{:S(2)}, u32[]{:S(2)}) collective-permute-start(f32[2,72,128]{2,1,0:T(8,128)S(1)} %fusion), channel_id=1, source_target_pairs={{0,2},{1,3},{2,0},{3,1},{4,6},{5,7},{6,4},{7,5},{8,10},{9,11},{10,... | collective-permute-start | bytes 221192 | tf_op jit(solution)/shard_map/ppermute | solution.py:37
  9.3 1.2 %collective-permute-start.3 = (f32[2,72,128]{2,1,0:T(8,128)S(1)}, f32[2,72,128]{2,1,0:T(8,128)S(1)}, u32[]{:S(2)}, u32[]{:S(2)}) collective-permute-start(f32[2,72,128]{2,1,0:T(8,128)S(1)} %fusion), channel_id=1, source_target_pairs={{0,4},{1,5},{2,6},{3,7},{4,0},{5,1},{6,2},{7,3},{8,12},{9,13},{10,... | collective-permute-start | bytes 221192 | tf_op jit(solution)/shard_map/ppermute | solution.py:37
  10.6 0.2 collective-permute-start.4
  10.7 0.8 %rsqrt.3 = f32[8192]{0:T(1024)S(1)} rsqrt(f32[8192]{0:T(1024)} %param.11) | non-fusion elementwise | bytes 65536 | tf_op jit(solution)/shard_map/rsqrt | solution.py:454
  11.5 0.0 copy-start
  11.5 0.0 copy-start.2
  11.5 0.0 copy-start.3
  11.6 4.2 %broadcast_multiply_fusion.basis_ref = f32[8192,128]{1,0:T(8,128)} fusion(f32[8192,128]{1,0:T(8,128)} %param.10, f32[8192]{0:T(1024)S(1)} %rsqrt.3), kind=kLoop, calls=%fused_computation | loop fusion | flops 1048576 | bytes 8421376 | tf_op jit(solution)/shard_map/mul | solution.py:454
  15.7 0.0 copy-start.1
  15.7 0.0 collective-permute-done.2
  15.7 0.0 collective-permute-done.3
  15.7 0.0 collective-permute-done.4
  15.8 3.0 %collective-permute-start.5 = (f32[8,72,128]{2,1,0:T(8,128)S(1)}, f32[8,72,128]{2,1,0:T(8,128)S(1)}, u32[]{:S(2)}, u32[]{:S(2)}) collective-permute-start(f32[8,72,128]{2,1,0:T(8,128)S(1)} %pad_maximum_fusion.refs_0_), channel_id=1, source_target_pairs={{0,1},{1,0},{2,3},{3,2},{4,5},{5,4},{6,7},{7,6},{8,9},{9,8},{10,11... | collective-permute-start | bytes 884744 | tf_op jit(solution)/shard_map/ppermute | solution.py:37
  18.7 0.0 copy-done
  18.7 0.0 copy-done.2
  18.7 0.0 copy-done.3
  18.7 2.7 %prepare.1 = (bf16[256,8192]{1,0:T(8,128)(2,1)S(1)}, bf16[8192,256]{1,0:T(8,128)(2,1)S(1)}, bf16[64,8192]{1,0:T(8,128)(2,1)S(1)}, f32[8,128]{1,0:T(8,128)S(1)}) custom-call(f32[8192,128]{1,0:T(8,128)} %broadcast_multiply_fusion.basis_ref, s32[1,8192]{1,0:T(1,128)S(1)} %bitcast.12, f32[1,128]{1,0:T(1,128)S(1)} %bitcast.14, f32[1,128]{1,0:T(1,128)S(1)} %bitcast.15), custom_call_target="tpu_custom_call" | custom-call | flops 2097152 | bytes 12582912 | tf_op jit(solution)/shard_map/prepare/pallas_call | solution.py:455
  21.4 0.0 collective-permute-done.5.refs_1_
  21.4 0.0 copy-done.1
  21.4 19.3 %filter.1 = (f32[1,8192]{1,0:T(1,128)}, f32[1,256]{1,0:T(1,128)}, f32[1,1]{1,0:T(1,128)}) custom-call(s32[1]{0:T(128)} %bitcast.position_ref, f32[8,72,128]{2,1,0:T(8,128)S(1)} %pad_maximum_fusion.refs_0_, f32[8,72,128]{2,1,0:T(8,128)S(1)} %collective-permute-done.5.refs_1_, bf16[64,8192]{1,0:T(8,128)(2,1)S(1)} %get-tuple-element.18.refs_2_, ...), custom_call_target="tpu_custom_call" | custom-call | flops 8589934592 | bytes 8388608 | tf_op jit(solution)/shard_map/filter/pallas_call | solution.py:461
  (4 shorter events, 0.0 us)
Async XLA Ops:
  0.6 6.7 %collective-permute-start = (f32[1,8192]{1,0:T(1,128)}, f32[1,8192]{1,0:T(1,128)S(1)}, u32[]{:S(2)}, u32[]{:S(2)}) collective-permute-start(f32[1,8192]{1,0:T(1,128)} %param.7), channel_id=1, source_target_pairs={{0,8},{1,9},{2,10},{3,11},{4,12},{5,13},{6,14},{7,15},{8,0},{9,1},... | collective-permute-start | bytes 98312 | tf_op jit(solution)/shard_map/ppermute | solution.py:37
  3.8 3.5 %collective-permute-start.1 = (s32[1,64]{1,0:T(1,128)}, s32[1,64]{1,0:T(1,128)S(1)}, u32[]{:S(2)}, u32[]{:S(2)}) collective-permute-start(s32[1,64]{1,0:T(1,128)} %param.8), channel_id=1, source_target_pairs={{0,8},{1,9},{2,10},{3,11},{4,12},{5,13},{6,14},{7,15},{8,0},{9,1},... | collective-permute-start | bytes 776 | tf_op jit(solution)/shard_map/ppermute | solution.py:37
  8.1 7.6 %collective-permute-start.2 = (f32[2,72,128]{2,1,0:T(8,128)S(1)}, f32[2,72,128]{2,1,0:T(8,128)S(1)}, u32[]{:S(2)}, u32[]{:S(2)}) collective-permute-start(f32[2,72,128]{2,1,0:T(8,128)S(1)} %fusion), channel_id=1, source_target_pairs={{0,2},{1,3},{2,0},{3,1},{4,6},{5,7},{6,4},{7,5},{8,10},{9,11},{10,... | collective-permute-start | bytes 221192 | tf_op jit(solution)/shard_map/ppermute | solution.py:37
  9.3 6.4 %collective-permute-start.3 = (f32[2,72,128]{2,1,0:T(8,128)S(1)}, f32[2,72,128]{2,1,0:T(8,128)S(1)}, u32[]{:S(2)}, u32[]{:S(2)}) collective-permute-start(f32[2,72,128]{2,1,0:T(8,128)S(1)} %fusion), channel_id=1, source_target_pairs={{0,4},{1,5},{2,6},{3,7},{4,0},{5,1},{6,2},{7,3},{8,12},{9,13},{10,... | collective-permute-start | bytes 221192 | tf_op jit(solution)/shard_map/ppermute | solution.py:37
  10.6 5.2 %collective-permute-start.4 = (f32[2,72,128]{2,1,0:T(8,128)S(1)}, f32[2,72,128]{2,1,0:T(8,128)S(1)}, u32[]{:S(2)}, u32[]{:S(2)}) collective-permute-start(f32[2,72,128]{2,1,0:T(8,128)S(1)} %fusion), channel_id=1, source_target_pairs={{0,6},{1,7},{2,4},{3,5},{4,2},{5,3},{6,0},{7,1},{8,14},{9,15},{10,... | collective-permute-start | bytes 221192 | tf_op jit(solution)/shard_map/ppermute | solution.py:37
  11.5 7.2 %copy-start = (s32[8192]{0:T(1024)S(1)}, s32[8192]{0:T(1024)}, u32[]{:S(2)}) copy-start(s32[8192]{0:T(1024)} %param.9) | copy-start | bytes 98308
  11.5 7.2 %copy-start.2 = (f32[128]{0:T(128)S(1)}, f32[128]{0:T(128)}, u32[]{:S(2)}) copy-start(f32[128]{0:T(128)} %param.12) | copy-start | bytes 1540
  11.5 7.2 %copy-start.3 = (f32[128]{0:T(128)S(1)}, f32[128]{0:T(128)}, u32[]{:S(2)}) copy-start(f32[128]{0:T(128)} %param.13) | copy-start | bytes 1540
  15.7 5.7 %copy-start.1 = (f32[8192]{0:T(1024)S(1)}, f32[8192]{0:T(1024)}, u32[]{:S(2)}) copy-start(f32[8192]{0:T(1024)} %param.11) | copy-start | bytes 98308
  15.8 5.6 %collective-permute-start.5 = (f32[8,72,128]{2,1,0:T(8,128)S(1)}, f32[8,72,128]{2,1,0:T(8,128)S(1)}, u32[]{:S(2)}, u32[]{:S(2)}) collective-permute-start(f32[8,72,128]{2,1,0:T(8,128)S(1)} %pad_maximum_fusion.refs_0_), channel_id=1, source_target_pairs={{0,1},{1,0},{2,3},{3,2},{4,5},{5,4},{6,7},{7,6},{8,9},{9,8},{10,11... | collective-permute-start | bytes 884744 | tf_op jit(solution)/shard_map/ppermute | solution.py:37

commit v6 on v4

--- a/solution.py
+++ b/solution.py
@@ -190,6 +190,7 @@
         pred_mean,
         columns,
         lam_now,
+        lam_split,
         root_ref,
         mask_rows,
         readings,
@@ -247,7 +248,9 @@
 
     def gram_finish(total):
         cross = total[:, modes:]
-        lam_now[...] = total[:, :modes] + cross + cross.T
+        lam = total[:, :modes] + cross + cross.T
+        lam_now[...] = lam
+        lam_split[...] = wide(lam)
 
     first_left = scaled_t_ref[:modes, :] * mask_rows[pl.ds(slot(0), 1), :].astype(BF16)
     y_high, y_low = split(readings[...])
@@ -263,7 +266,7 @@
         pred_vv = p_vv[...]
         pred_rv = p_rv[...]
         pred_rr = p_rr[...]
-        lam_wide = wide(lam)
+        lam_wide = lam_split[...]
         lam_p = dot_three(lam_wide, pred_vv)
         cross = dot_three(lam_wide, p_vr[...])
         total = None if last else gram_piece(0, ahead) + gram_piece(1, ahead)
@@ -475,6 +478,7 @@
             pltpu.VMEM((2, modes, modes), F32),
             pltpu.VMEM((4, modes, modes), F32),
             square,
+            pltpu.VMEM((modes, 2 * modes), BF16),
             pltpu.VMEM((1, sensors), F32),
             pltpu.VMEM((steps, sensors), F32),
             pltpu.VMEM((steps, sensors), F32),

time: 41.1 us -> 41.1 us (level)
  no operation moved by 1% of the time
where the time goes in v6:
time: 41.1 us; the launch traced here: 40.9 us
  Pallas kernels  22.1 us (54%)
  starting transfers between devices  8.88 us (22%)
  other arithmetic  5.65 us (14%)
  waiting for transfers between devices  2.72 us (7%)
  local copies, waits for them, and re-layouts  0.8 us (2%)
  between operations  0.71 us (2%)
    pallas_call x1, Pallas kernels, on_device(): pl.pallas_call(functools.partial(filter_kernel, count=count, local=local,...  19.3 us
    ppermute x6, starting transfers between devices, swap(): return lax.ppermute(array, AXIS, [(p, p ^ flip) for p in range(count)])  8.88 us
    mul x1, other arithmetic, on_device(): sensor_basis * lax.rsqrt(noise)[:, None]  4.17 us
    pallas_call x1, Pallas kernels, on_device(): prepare(scaled, block_row, rate_row, var_row)  2.78 us
    ppermute x6, waiting for transfers between devices, swap(): return lax.ppermute(array, AXIS, [(p, p ^ flip) for p in range(count)])  2.72 us
  transfers between devices with their start and end apart: 6, of which 1 were waited for; matrix products, arithmetic and copies ran while one was open for 14% of the time, Pallas kernels for 7%

profile of v6, /device:TPU:1, one launch (start us, length us, event | category | flops | bytes accessed | tf_op | source)
XLA Modules:
  0.0 40.9 jit_solution(9841576598493865308)
XLA Ops:
  0.6 3.2 %collective-permute-start = (f32[1,8192]{1,0:T(1,128)}, f32[1,8192]{1,0:T(1,128)S(1)}, u32[]{:S(2)}, u32[]{:S(2)}) collective-permute-start(f32[1,8192]{1,0:T(1,128)} %param.7), channel_id=1, source_target_pairs={{0,8},{1,9},{2,10},{3,11},{4,12},{5,13},{6,14},{7,15},{8,0},{9,1},... | collective-permute-start | bytes 98312 | tf_op jit(solution)/shard_map/ppermute | solution.py:37
  3.8 0.1 collective-permute-start.1
  3.9 0.7 %convert_element_type.12 = f32[1,64]{1,0:T(1,128)S(1)} convert(s32[1,64]{1,0:T(1,128)} %param.8) | non-fusion elementwise | flops 64 | bytes 512 | tf_op jit(solution)/shard_map/convert_element_type | solution.py:42
  4.6 2.7 %collective-permute-done.1 = s32[1,64]{1,0:T(1,128)S(1)} collective-permute-done((s32[1,64]{1,0:T(1,128)}, s32[1,64]{1,0:T(1,128)S(1)}, u32[]{:S(2)}, u32[]{:S(2)}) %collective-permute-start.1) | collective-permute-done | bytes 288 | tf_op jit(solution)/shard_map/ppermute | solution.py:37
  7.3 0.0 collective-permute-done
  7.3 0.8 %fusion = f32[2,72,128]{2,1,0:T(8,128)S(1)} fusion(f32[1,1,128]{2,1,0:T(1,128)S(1)} %pad_bitcast_fusion, f32[1,1,128]{2,1,0:T(1,128)S(1)} %pad_bitcast_fusion.1, f32[1,64,128]{2,1,0:T(8,128)S(1)} %bitcast.17, f32[1,64,128]{2,1,0:T(8,128)} %bitcast.16), kind=kLoop, calls=%fused_computation.3 | loop fusion | flops 221184 | bytes 140288 | tf_op jit(solution)/shard_map/concatenate | solution.py:53
  8.1 1.2 %collective-permute-start.2 = (f32[2,72,128]{2,1,0:T(8,128)S(1)}, f32[2,72,128]{2,1,0:T(8,128)S(1)}, u32[]{:S(2)}, u32[]{:S(2)}) collective-permute-start(f32[2,72,128]{2,1,0:T(8,128)S(1)} %fusion), channel_id=1, source_target_pairs={{0,2},{1,3},{2,0},{3,1},{4,6},{5,7},{6,4},{7,5},{8,10},{9,11},{10,... | collective-permute-start | bytes 221192 | tf_op jit(solution)/shard_map/ppermute | solution.py:37
  9.3 1.2 %collective-permute-start.3 = (f32[2,72,128]{2,1,0:T(8,128)S(1)}, f32[2,72,128]{2,1,0:T(8,128)S(1)}, u32[]{:S(2)}, u32[]{:S(2)}) collective-permute-start(f32[2,72,128]{2,1,0:T(8,128)S(1)} %fusion), channel_id=1, source_target_pairs={{0,4},{1,5},{2,6},{3,7},{4,0},{5,1},{6,2},{7,3},{8,12},{9,13},{10,... | collective-permute-start | bytes 221192 | tf_op jit(solution)/shard_map/ppermute | solution.py:37
  10.6 0.2 collective-permute-start.4
  10.7 0.8 %rsqrt.3 = f32[8192]{0:T(1024)S(1)} rsqrt(f32[8192]{0:T(1024)} %param.11) | non-fusion elementwise | bytes 65536 | tf_op jit(solution)/shard_map/rsqrt | solution.py:457
  11.5 0.0 copy-start
  11.5 0.0 copy-start.2
  11.5 0.0 copy-start.3
  11.6 4.2 %broadcast_multiply_fusion.basis_ref = f32[8192,128]{1,0:T(8,128)} fusion(f32[8192,128]{1,0:T(8,128)} %param.10, f32[8192]{0:T(1024)S(1)} %rsqrt.3), kind=kLoop, calls=%fused_computation | loop fusion | flops 1048576 | bytes 8421376 | tf_op jit(solution)/shard_map/mul | solution.py:457
  15.7 0.0 copy-start.1
  15.7 0.0 collective-permute-done.2
  15.7 0.0 collective-permute-done.3
  15.7 0.0 collective-permute-done.4
  15.8 3.0 %collective-permute-start.5 = (f32[8,72,128]{2,1,0:T(8,128)S(1)}, f32[8,72,128]{2,1,0:T(8,128)S(1)}, u32[]{:S(2)}, u32[]{:S(2)}) collective-permute-start(f32[8,72,128]{2,1,0:T(8,128)S(1)} %pad_maximum_fusion.refs_0_), channel_id=1, source_target_pairs={{0,1},{1,0},{2,3},{3,2},{4,5},{5,4},{6,7},{7,6},{8,9},{9,8},{10,11... | collective-permute-start | bytes 884744 | tf_op jit(solution)/shard_map/ppermute | solution.py:37
  18.7 0.0 copy-done
  18.7 0.0 copy-done.2
  18.7 0.0 copy-done.3
  18.7 2.8 %prepare.1 = (bf16[256,8192]{1,0:T(8,128)(2,1)S(1)}, bf16[8192,256]{1,0:T(8,128)(2,1)S(1)}, bf16[64,8192]{1,0:T(8,128)(2,1)S(1)}, f32[8,128]{1,0:T(8,128)S(1)}) custom-call(f32[8192,128]{1,0:T(8,128)} %broadcast_multiply_fusion.basis_ref, s32[1,8192]{1,0:T(1,128)S(1)} %bitcast.12, f32[1,128]{1,0:T(1,128)S(1)} %bitcast.14, f32[1,128]{1,0:T(1,128)S(1)} %bitcast.15), custom_call_target="tpu_custom_call" | custom-call | flops 2097152 | bytes 12582912 | tf_op jit(solution)/shard_map/prepare/pallas_call | solution.py:458
  21.5 0.0 collective-permute-done.5.refs_1_
  21.5 0.0 copy-done.1
  21.5 19.3 %filter.1 = (f32[1,8192]{1,0:T(1,128)}, f32[1,256]{1,0:T(1,128)}, f32[1,1]{1,0:T(1,128)}) custom-call(s32[1]{0:T(128)} %bitcast.position_ref, f32[8,72,128]{2,1,0:T(8,128)S(1)} %pad_maximum_fusion.refs_0_, f32[8,72,128]{2,1,0:T(8,128)S(1)} %collective-permute-done.5.refs_1_, bf16[64,8192]{1,0:T(8,128)(2,1)S(1)} %get-tuple-element.18.refs_2_, ...), custom_call_target="tpu_custom_call" | custom-call | flops 8589934592 | bytes 8388608 | tf_op jit(solution)/shard_map/filter/pallas_call | solution.py:464
  (4 shorter events, 0.0 us)
Async XLA Ops:
  0.6 6.7 %collective-permute-start = (f32[1,8192]{1,0:T(1,128)}, f32[1,8192]{1,0:T(1,128)S(1)}, u32[]{:S(2)}, u32[]{:S(2)}) collective-permute-start(f32[1,8192]{1,0:T(1,128)} %param.7), channel_id=1, source_target_pairs={{0,8},{1,9},{2,10},{3,11},{4,12},{5,13},{6,14},{7,15},{8,0},{9,1},... | collective-permute-start | bytes 98312 | tf_op jit(solution)/shard_map/ppermute | solution.py:37
  3.8 3.5 %collective-permute-start.1 = (s32[1,64]{1,0:T(1,128)}, s32[1,64]{1,0:T(1,128)S(1)}, u32[]{:S(2)}, u32[]{:S(2)}) collective-permute-start(s32[1,64]{1,0:T(1,128)} %param.8), channel_id=1, source_target_pairs={{0,8},{1,9},{2,10},{3,11},{4,12},{5,13},{6,14},{7,15},{8,0},{9,1},... | collective-permute-start | bytes 776 | tf_op jit(solution)/shard_map/ppermute | solution.py:37
  8.1 7.6 %collective-permute-start.2 = (f32[2,72,128]{2,1,0:T(8,128)S(1)}, f32[2,72,128]{2,1,0:T(8,128)S(1)}, u32[]{:S(2)}, u32[]{:S(2)}) collective-permute-start(f32[2,72,128]{2,1,0:T(8,128)S(1)} %fusion), channel_id=1, source_target_pairs={{0,2},{1,3},{2,0},{3,1},{4,6},{5,7},{6,4},{7,5},{8,10},{9,11},{10,... | collective-permute-start | bytes 221192 | tf_op jit(solution)/shard_map/ppermute | solution.py:37
  9.3 6.4 %collective-permute-start.3 = (f32[2,72,128]{2,1,0:T(8,128)S(1)}, f32[2,72,128]{2,1,0:T(8,128)S(1)}, u32[]{:S(2)}, u32[]{:S(2)}) collective-permute-start(f32[2,72,128]{2,1,0:T(8,128)S(1)} %fusion), channel_id=1, source_target_pairs={{0,4},{1,5},{2,6},{3,7},{4,0},{5,1},{6,2},{7,3},{8,12},{9,13},{10,... | collective-permute-start | bytes 221192 | tf_op jit(solution)/shard_map/ppermute | solution.py:37
  10.6 5.2 %collective-permute-start.4 = (f32[2,72,128]{2,1,0:T(8,128)S(1)}, f32[2,72,128]{2,1,0:T(8,128)S(1)}, u32[]{:S(2)}, u32[]{:S(2)}) collective-permute-start(f32[2,72,128]{2,1,0:T(8,128)S(1)} %fusion), channel_id=1, source_target_pairs={{0,6},{1,7},{2,4},{3,5},{4,2},{5,3},{6,0},{7,1},{8,14},{9,15},{10,... | collective-permute-start | bytes 221192 | tf_op jit(solution)/shard_map/ppermute | solution.py:37
  11.5 7.2 %copy-start = (s32[8192]{0:T(1024)S(1)}, s32[8192]{0:T(1024)}, u32[]{:S(2)}) copy-start(s32[8192]{0:T(1024)} %param.9) | copy-start | bytes 98308
  11.5 7.2 %copy-start.2 = (f32[128]{0:T(128)S(1)}, f32[128]{0:T(128)}, u32[]{:S(2)}) copy-start(f32[128]{0:T(128)} %param.12) | copy-start | bytes 1540
  11.5 7.2 %copy-start.3 = (f32[128]{0:T(128)S(1)}, f32[128]{0:T(128)}, u32[]{:S(2)}) copy-start(f32[128]{0:T(128)} %param.13) | copy-start | bytes 1540
  15.7 5.8 %copy-start.1 = (f32[8192]{0:T(1024)S(1)}, f32[8192]{0:T(1024)}, u32[]{:S(2)}) copy-start(f32[8192]{0:T(1024)} %param.11) | copy-start | bytes 98308
  15.8 5.7 %collective-permute-start.5 = (f32[8,72,128]{2,1,0:T(8,128)S(1)}, f32[8,72,128]{2,1,0:T(8,128)S(1)}, u32[]{:S(2)}, u32[]{:S(2)}) collective-permute-start(f32[8,72,128]{2,1,0:T(8,128)S(1)} %pad_maximum_fusion.refs_0_), channel_id=1, source_target_pairs={{0,1},{1,0},{2,3},{3,2},{4,5},{5,4},{6,7},{7,6},{8,9},{9,8},{10,11... | collective-permute-start | bytes 884744 | tf_op jit(solution)/shard_map/ppermute | solution.py:37

commit v7 on v4

--- a/solution.py
+++ b/solution.py
@@ -403,11 +403,11 @@
     scaled_field = f_both[:steps] + f_both[steps:]
     field_ref[...] = scaled_field[:local] * (root_ref[...] * noise_ref[...])
     variances_ref[...] = diagonals[:local, :]
-    gap = readings[...] - mask_rows[...] * scaled_field
-    squares = gap * gap
-    lanes_first = squares[:, :LANES]
-    for chunk in range(1, chunks):
-        lanes_first = lanes_first + squares[:, chunk * LANES : (chunk + 1) * LANES]
+    lanes_first = jnp.zeros((steps, LANES), F32)
+    for chunk in range(chunks):
+        span = slice(chunk * LANES, (chunk + 1) * LANES)
+        gap = readings[:, span] - mask_rows[:, span] * scaled_field[:, span]
+        lanes_first = lanes_first + gap * gap
     row_sums[...] = lanes_first
     lane_total = row_sums[pl.ds(slot(0), 1), :]
     for step in range(1, steps):

time: 41.1 us -> 41.1 us (level)
  no operation moved by 1% of the time
where the time goes in v7:
time: 41.1 us; the launch traced here: 40.8 us
  Pallas kernels  22 us (54%)
  starting transfers between devices  8.88 us (22%)
  other arithmetic  5.65 us (14%)
  waiting for transfers between devices  2.72 us (7%)
  local copies, waits for them, and re-layouts  0.8 us (2%)
  between operations  0.71 us (2%)
    pallas_call x1, Pallas kernels, on_device(): pl.pallas_call(functools.partial(filter_kernel, count=count, local=local,...  19.3 us
    ppermute x6, starting transfers between devices, swap(): return lax.ppermute(array, AXIS, [(p, p ^ flip) for p in range(count)])  8.88 us
    mul x1, other arithmetic, on_device(): sensor_basis * lax.rsqrt(noise)[:, None]  4.17 us
    pallas_call x1, Pallas kernels, on_device(): prepare(scaled, block_row, rate_row, var_row)  2.78 us
    ppermute x6, waiting for transfers between devices, swap(): return lax.ppermute(array, AXIS, [(p, p ^ flip) for p in range(count)])  2.72 us
  transfers between devices with their start and end apart: 6, of which 1 were waited for; matrix products, arithmetic and copies ran while one was open for 14% of the time, Pallas kernels for 7%

profile of v7, /device:TPU:1, one launch (start us, length us, event | category | flops | bytes accessed | tf_op | source)
XLA Modules:
  0.0 40.8 jit_solution(17345711655988479673)
XLA Ops:
  0.6 3.2 %collective-permute-start = (f32[1,8192]{1,0:T(1,128)}, f32[1,8192]{1,0:T(1,128)S(1)}, u32[]{:S(2)}, u32[]{:S(2)}) collective-permute-start(f32[1,8192]{1,0:T(1,128)} %param.7), channel_id=1, source_target_pairs={{0,8},{1,9},{2,10},{3,11},{4,12},{5,13},{6,14},{7,15},{8,0},{9,1},... | collective-permute-start | bytes 98312 | tf_op jit(solution)/shard_map/ppermute | solution.py:37
  3.8 0.1 collective-permute-start.1
  3.9 0.7 %convert_element_type.12 = f32[1,64]{1,0:T(1,128)S(1)} convert(s32[1,64]{1,0:T(1,128)} %param.8) | non-fusion elementwise | flops 64 | bytes 512 | tf_op jit(solution)/shard_map/convert_element_type | solution.py:42
  4.6 2.7 %collective-permute-done.1 = s32[1,64]{1,0:T(1,128)S(1)} collective-permute-done((s32[1,64]{1,0:T(1,128)}, s32[1,64]{1,0:T(1,128)S(1)}, u32[]{:S(2)}, u32[]{:S(2)}) %collective-permute-start.1) | collective-permute-done | bytes 288 | tf_op jit(solution)/shard_map/ppermute | solution.py:37
  7.3 0.0 collective-permute-done
  7.3 0.8 %fusion = f32[2,72,128]{2,1,0:T(8,128)S(1)} fusion(f32[1,1,128]{2,1,0:T(1,128)S(1)} %pad_bitcast_fusion, f32[1,1,128]{2,1,0:T(1,128)S(1)} %pad_bitcast_fusion.1, f32[1,64,128]{2,1,0:T(8,128)S(1)} %bitcast.17, f32[1,64,128]{2,1,0:T(8,128)} %bitcast.16), kind=kLoop, calls=%fused_computation.3 | loop fusion | flops 221184 | bytes 140288 | tf_op jit(solution)/shard_map/concatenate | solution.py:53
  8.1 1.2 %collective-permute-start.2 = (f32[2,72,128]{2,1,0:T(8,128)S(1)}, f32[2,72,128]{2,1,0:T(8,128)S(1)}, u32[]{:S(2)}, u32[]{:S(2)}) collective-permute-start(f32[2,72,128]{2,1,0:T(8,128)S(1)} %fusion), channel_id=1, source_target_pairs={{0,2},{1,3},{2,0},{3,1},{4,6},{5,7},{6,4},{7,5},{8,10},{9,11},{10,... | collective-permute-start | bytes 221192 | tf_op jit(solution)/shard_map/ppermute | solution.py:37
  9.3 1.2 %collective-permute-start.3 = (f32[2,72,128]{2,1,0:T(8,128)S(1)}, f32[2,72,128]{2,1,0:T(8,128)S(1)}, u32[]{:S(2)}, u32[]{:S(2)}) collective-permute-start(f32[2,72,128]{2,1,0:T(8,128)S(1)} %fusion), channel_id=1, source_target_pairs={{0,4},{1,5},{2,6},{3,7},{4,0},{5,1},{6,2},{7,3},{8,12},{9,13},{10,... | collective-permute-start | bytes 221192 | tf_op jit(solution)/shard_map/ppermute | solution.py:37
  10.6 0.2 collective-permute-start.4
  10.7 0.8 %rsqrt.3 = f32[8192]{0:T(1024)S(1)} rsqrt(f32[8192]{0:T(1024)} %param.11) | non-fusion elementwise | bytes 65536 | tf_op jit(solution)/shard_map/rsqrt | solution.py:454
  11.5 0.0 copy-start
  11.5 0.0 copy-start.2
  11.5 0.0 copy-start.3
  11.6 4.2 %broadcast_multiply_fusion.basis_ref = f32[8192,128]{1,0:T(8,128)} fusion(f32[8192,128]{1,0:T(8,128)} %param.10, f32[8192]{0:T(1024)S(1)} %rsqrt.3), kind=kLoop, calls=%fused_computation | loop fusion | flops 1048576 | bytes 8421376 | tf_op jit(solution)/shard_map/mul | solution.py:454
  15.7 0.0 copy-start.1
  15.7 0.0 collective-permute-done.2
  15.7 0.0 collective-permute-done.3
  15.7 0.0 collective-permute-done.4
  15.8 3.0 %collective-permute-start.5 = (f32[8,72,128]{2,1,0:T(8,128)S(1)}, f32[8,72,128]{2,1,0:T(8,128)S(1)}, u32[]{:S(2)}, u32[]{:S(2)}) collective-permute-start(f32[8,72,128]{2,1,0:T(8,128)S(1)} %pad_maximum_fusion.refs_0_), channel_id=1, source_target_pairs={{0,1},{1,0},{2,3},{3,2},{4,5},{5,4},{6,7},{7,6},{8,9},{9,8},{10,11... | collective-permute-start | bytes 884744 | tf_op jit(solution)/shard_map/ppermute | solution.py:37
  18.7 0.0 copy-done
  18.7 0.0 copy-done.2
  18.7 0.0 copy-done.3
  18.7 2.8 %prepare.1 = (bf16[256,8192]{1,0:T(8,128)(2,1)S(1)}, bf16[8192,256]{1,0:T(8,128)(2,1)S(1)}, bf16[64,8192]{1,0:T(8,128)(2,1)S(1)}, f32[8,128]{1,0:T(8,128)S(1)}) custom-call(f32[8192,128]{1,0:T(8,128)} %broadcast_multiply_fusion.basis_ref, s32[1,8192]{1,0:T(1,128)S(1)} %bitcast.12, f32[1,128]{1,0:T(1,128)S(1)} %bitcast.14, f32[1,128]{1,0:T(1,128)S(1)} %bitcast.15), custom_call_target="tpu_custom_call" | custom-call | flops 2097152 | bytes 12582912 | tf_op jit(solution)/shard_map/prepare/pallas_call | solution.py:455
  21.5 0.0 collective-permute-done.5.refs_1_
  21.5 0.0 copy-done.1
  21.5 19.3 %filter.1 = (f32[1,8192]{1,0:T(1,128)}, f32[1,256]{1,0:T(1,128)}, f32[1,1]{1,0:T(1,128)}) custom-call(s32[1]{0:T(128)} %bitcast.position_ref, f32[8,72,128]{2,1,0:T(8,128)S(1)} %pad_maximum_fusion.refs_0_, f32[8,72,128]{2,1,0:T(8,128)S(1)} %collective-permute-done.5.refs_1_, bf16[64,8192]{1,0:T(8,128)(2,1)S(1)} %get-tuple-element.18.refs_2_, ...), custom_call_target="tpu_custom_call" | custom-call | flops 8589934592 | bytes 8388608 | tf_op jit(solution)/shard_map/filter/pallas_call | solution.py:461
  (4 shorter events, 0.0 us)
Async XLA Ops:
  0.6 6.7 %collective-permute-start = (f32[1,8192]{1,0:T(1,128)}, f32[1,8192]{1,0:T(1,128)S(1)}, u32[]{:S(2)}, u32[]{:S(2)}) collective-permute-start(f32[1,8192]{1,0:T(1,128)} %param.7), channel_id=1, source_target_pairs={{0,8},{1,9},{2,10},{3,11},{4,12},{5,13},{6,14},{7,15},{8,0},{9,1},... | collective-permute-start | bytes 98312 | tf_op jit(solution)/shard_map/ppermute | solution.py:37
  3.8 3.5 %collective-permute-start.1 = (s32[1,64]{1,0:T(1,128)}, s32[1,64]{1,0:T(1,128)S(1)}, u32[]{:S(2)}, u32[]{:S(2)}) collective-permute-start(s32[1,64]{1,0:T(1,128)} %param.8), channel_id=1, source_target_pairs={{0,8},{1,9},{2,10},{3,11},{4,12},{5,13},{6,14},{7,15},{8,0},{9,1},... | collective-permute-start | bytes 776 | tf_op jit(solution)/shard_map/ppermute | solution.py:37
  8.1 7.6 %collective-permute-start.2 = (f32[2,72,128]{2,1,0:T(8,128)S(1)}, f32[2,72,128]{2,1,0:T(8,128)S(1)}, u32[]{:S(2)}, u32[]{:S(2)}) collective-permute-start(f32[2,72,128]{2,1,0:T(8,128)S(1)} %fusion), channel_id=1, source_target_pairs={{0,2},{1,3},{2,0},{3,1},{4,6},{5,7},{6,4},{7,5},{8,10},{9,11},{10,... | collective-permute-start | bytes 221192 | tf_op jit(solution)/shard_map/ppermute | solution.py:37
  9.3 6.4 %collective-permute-start.3 = (f32[2,72,128]{2,1,0:T(8,128)S(1)}, f32[2,72,128]{2,1,0:T(8,128)S(1)}, u32[]{:S(2)}, u32[]{:S(2)}) collective-permute-start(f32[2,72,128]{2,1,0:T(8,128)S(1)} %fusion), channel_id=1, source_target_pairs={{0,4},{1,5},{2,6},{3,7},{4,0},{5,1},{6,2},{7,3},{8,12},{9,13},{10,... | collective-permute-start | bytes 221192 | tf_op jit(solution)/shard_map/ppermute | solution.py:37
  10.6 5.2 %collective-permute-start.4 = (f32[2,72,128]{2,1,0:T(8,128)S(1)}, f32[2,72,128]{2,1,0:T(8,128)S(1)}, u32[]{:S(2)}, u32[]{:S(2)}) collective-permute-start(f32[2,72,128]{2,1,0:T(8,128)S(1)} %fusion), channel_id=1, source_target_pairs={{0,6},{1,7},{2,4},{3,5},{4,2},{5,3},{6,0},{7,1},{8,14},{9,15},{10,... | collective-permute-start | bytes 221192 | tf_op jit(solution)/shard_map/ppermute | solution.py:37
  11.5 7.2 %copy-start = (s32[8192]{0:T(1024)S(1)}, s32[8192]{0:T(1024)}, u32[]{:S(2)}) copy-start(s32[8192]{0:T(1024)} %param.9) | copy-start | bytes 98308
  11.5 7.2 %copy-start.2 = (f32[128]{0:T(128)S(1)}, f32[128]{0:T(128)}, u32[]{:S(2)}) copy-start(f32[128]{0:T(128)} %param.12) | copy-start | bytes 1540
  11.5 7.2 %copy-start.3 = (f32[128]{0:T(128)S(1)}, f32[128]{0:T(128)}, u32[]{:S(2)}) copy-start(f32[128]{0:T(128)} %param.13) | copy-start | bytes 1540
  15.7 5.8 %copy-start.1 = (f32[8192]{0:T(1024)S(1)}, f32[8192]{0:T(1024)}, u32[]{:S(2)}) copy-start(f32[8192]{0:T(1024)} %param.11) | copy-start | bytes 98308
  15.8 5.7 %collective-permute-start.5 = (f32[8,72,128]{2,1,0:T(8,128)S(1)}, f32[8,72,128]{2,1,0:T(8,128)S(1)}, u32[]{:S(2)}, u32[]{:S(2)}) collective-permute-start(f32[8,72,128]{2,1,0:T(8,128)S(1)} %pad_maximum_fusion.refs_0_), channel_id=1, source_target_pairs={{0,1},{1,0},{2,3},{3,2},{4,5},{5,4},{6,7},{7,6},{8,9},{9,8},{10,11... | collective-permute-start | bytes 884744 | tf_op jit(solution)/shard_map/ppermute | solution.py:37
